TPU v7x, 32 devices: a whole 2x2x4 slice. The times are simulated.
32 devices in a mesh: dp: 4 (over y, core), seq: 8 (over z, x).
Axes of the slice: x: 2, y: 2, z: 4, core: 2. Of those that a mesh axis runs over, the one named last changes fastest.
Arguments:
- inputs: bfloat16 [4, 2048, 1024], P('dp', 'seq'), may hold values from -6 to 6
- cotangent: bfloat16 [4, 2048, 1024], P('dp', 'seq'), may hold values from -6 to 6
- context: int32 [4], P('dp'), may hold values from 1 to 7
- levels: int32 [4, 8], P('dp', 'seq'), may hold values from 1 to 999
- w_qkv: bfloat16 [1024, 3072], P(('dp', 'seq')), may hold values from -0.1875 to 0.1875
- b_qkv: bfloat16 [3072], P(('dp', 'seq')), may hold values from -3 to 3
- w_out: bfloat16 [1024, 1024], P(('dp', 'seq')), may hold values from -3 to 3
- b_out: bfloat16 [1024], P(('dp', 'seq')), may hold values from -3 to 3
- w_up: bfloat16 [1024, 4096], P(('dp', 'seq')), may hold values from -0.1875 to 0.1875
- b_up: bfloat16 [4096], P(('dp', 'seq')), may hold values from -3 to 3
- w_down: bfloat16 [4096, 1024], P(('dp', 'seq')), may hold values from -0.09375 to 0.09375
- b_down: bfloat16 [1024], P(('dp', 'seq')), may hold values from -3 to 3
- w_mod: bfloat16 [1024, 6144], P(('dp', 'seq')), may hold values from -0.1875 to 0.1875
- b_mod: bfloat16 [6144], P(('dp', 'seq')), may hold values from -3 to 3
Outputs:
- layer_out: bfloat16 [4, 2048, 1024], P('dp', 'seq')
- input_grad: bfloat16 [4, 2048, 1024], P('dp', 'seq')
- g_wqkv: float32 [1024, 3072], P(('dp', 'seq'))
- g_bqkv: float32 [3072], P(('dp', 'seq'))
- g_wout: float32 [1024, 1024], P(('dp', 'seq'))
- g_bout: float32 [1024], P(('dp', 'seq'))
- g_wup: float32 [1024, 4096], P(('dp', 'seq'))
- g_bup: float32 [4096], P(('dp', 'seq'))
- g_wdown: float32 [4096, 1024], P(('dp', 'seq'))
- g_bdown: float32 [1024], P(('dp', 'seq'))
- g_wmod: float32 [1024, 6144], P(('dp', 'seq'))
- g_bmod: float32 [6144], P(('dp', 'seq'))
All inputs are finite; a program needn't handle non-finite values.
Results may differ from a plain program's by a relative error of at most 0.017.
Values may be sent and summed in bfloat16 or wider, within the bound.
No kernel may reach another device: no remote copies, remote signals or barrier semaphores. Data moves between devices by JAX's collectives and lax.ppermute only.
A program may use at most 256 MiB of HBM per device.

v0:
```python
import math

import jax
import jax.numpy as jnp
from jax import lax
from jax.sharding import PartitionSpec as P

D = 1024
H = 16
HD = 64
PW = 16


eps = 1e-06


def layer_norm(values):
    row_mean = jnp.mean(values, axis=-1, keepdims=True)
    centred = values - row_mean
    inv_std = lax.rsqrt(jnp.mean(centred * centred, axis=-1, keepdims=True) + eps)
    return (centred * inv_std, inv_std)


def norm_back(normed, inv_std, normed_grad):
    first_mean = jnp.mean(normed_grad, axis=-1, keepdims=True)
    second_mean = jnp.mean(normed_grad * normed, axis=-1, keepdims=True)
    return inv_std * (normed_grad - first_mean - normed * second_mean)


def level_embedding(effective, width):
    half_width = width // 2
    frequency = jnp.exp(
        -math.log(10000.0) * jnp.arange(half_width).astype(jnp.float32) / half_width
    )
    angles = effective.astype(jnp.float32)[..., None] * frequency
    return jnp.concatenate([jnp.cos(angles), jnp.sin(angles)], axis=-1)


def rope_angles(frame_pos, row_pos, column_pos, head_width):
    pair_count = head_width // 2
    time_pairs = head_width // 8
    space_pairs = 3 * head_width // 16
    pair_index = jnp.arange(pair_count)
    axis_pick = jnp.where(
        pair_index < time_pairs, 0, jnp.where(pair_index < time_pairs + space_pairs, 1, 2)
    )
    local_rank = jnp.where(
        axis_pick == 0,
        pair_index,
        jnp.where(axis_pick == 1, pair_index - time_pairs, pair_index - time_pairs - space_pairs),
    )
    group_size = jnp.where(axis_pick == 0, time_pairs, space_pairs)
    frequency = jnp.exp(
        -math.log(10000.0) * local_rank.astype(jnp.float32) / group_size.astype(jnp.float32)
    )
    position = jnp.where(
        axis_pick == 0,
        frame_pos[:, None],
        jnp.where(axis_pick == 1, row_pos[:, None], column_pos[:, None]),
    )
    return position.astype(jnp.float32) * frequency


def rotate(values, cosine, sine_table):
    half_width = values.shape[-1] // 2
    first_half = values[..., :half_width]
    second_half = values[..., half_width:]
    cos_b = cosine[:, None, :]
    sin_b = sine_table[:, None, :]
    return jnp.concatenate(
        [first_half * cos_b - second_half * sin_b, first_half * sin_b + second_half * cos_b],
        axis=-1,
    )


def unrotate(grads, cosine, sine_table):
    half_width = grads.shape[-1] // 2
    first_half = grads[..., :half_width]
    second_half = grads[..., half_width:]
    cos_b = cosine[:, None, :]
    sin_b = sine_table[:, None, :]
    return jnp.concatenate(
        [first_half * cos_b + second_half * sin_b, second_half * cos_b - first_half * sin_b],
        axis=-1,
    )


def gelu_tanh(values):
    return jax.nn.gelu(values, approximate=True)


def outer_sum(left, right):
    return lax.dot_general(
        left, right, (((0,), (0,)), ((), ())), preferred_element_type=jnp.float32
    )


def back_dot(grads, weight):
    return lax.dot_general(
        grads, weight, (((1,), (1,)), ((), ())), preferred_element_type=jnp.float32
    )


def add_rows(buffer, part, offset):
    current = lax.dynamic_slice_in_dim(buffer, offset, part.shape[1], 1)
    return lax.dynamic_update_slice_in_dim(buffer, current + part, offset, 1)


def take_block(flat_rows, offset, block_rows, head_count, head_width):
    block = lax.dynamic_slice_in_dim(flat_rows, offset, block_rows, 1)
    return block.reshape(block.shape[0], block_rows, head_count, head_width)


def attend_rows(queries, key_flat, value_flat, key_frames, block_rows):
    clip_count, row_count, head_count, head_width = queries.shape
    score_scale = 1.0 / math.sqrt(head_width)

    def key_step(block_index, carry):
        running_max, running_sum, accumulated = carry
        key_block = take_block(
            key_flat, block_index * block_rows, block_rows, head_count, head_width
        )
        value_block = take_block(
            value_flat, block_index * block_rows, block_rows, head_count, head_width
        )
        scores = (
            jnp.einsum("cqhd,ckhd->chqk", queries, key_block, preferred_element_type=jnp.float32)
            * score_scale
        )
        new_max = jnp.maximum(running_max, jnp.max(scores, axis=-1))
        shrink = jnp.exp(running_max - new_max)
        weights = jnp.exp(scores - new_max[..., None])
        running_sum = running_sum * shrink + jnp.sum(weights, axis=-1)
        accumulated = accumulated * shrink[..., None] + jnp.einsum(
            "chqk,ckhd->chqd",
            weights.astype(jnp.bfloat16),
            value_block,
            preferred_element_type=jnp.float32,
        )
        return (new_max, running_sum, accumulated)

    initial = (
        jnp.full((clip_count, head_count, row_count), -1e30, jnp.float32),
        jnp.zeros((clip_count, head_count, row_count), jnp.float32),
        jnp.zeros((clip_count, head_count, row_count, head_width), jnp.float32),
    )
    running_max, running_sum, accumulated = lax.fori_loop(0, key_frames, key_step, initial)
    attended = jnp.transpose(accumulated / running_sum[..., None], (0, 2, 1, 3))
    return (attended, running_max + jnp.log(running_sum))


def attend_back(
    queries,
    key_flat,
    value_flat,
    grad_out,
    out_rows,
    lse_rows,
    key_frames,
    block_rows,
    key_grads,
    value_grads,
):
    clip_count, row_count, head_count, head_width = queries.shape
    score_scale = 1.0 / math.sqrt(head_width)
    delta = jnp.transpose(jnp.sum(grad_out.astype(jnp.float32) * out_rows, axis=-1), (0, 2, 1))

    def key_step(block_index, carry):
        query_grad, key_grads, value_grads = carry
        offset = block_index * block_rows
        key_block = take_block(key_flat, offset, block_rows, head_count, head_width)
        value_block = take_block(value_flat, offset, block_rows, head_count, head_width)
        scores = (
            jnp.einsum("cqhd,ckhd->chqk", queries, key_block, preferred_element_type=jnp.float32)
            * score_scale
        )
        probs = jnp.exp(scores - lse_rows[..., None])
        value_part = jnp.einsum(
            "chqk,cqhd->ckhd",
            probs.astype(jnp.bfloat16),
            grad_out,
            preferred_element_type=jnp.float32,
        )
        prob_grad = jnp.einsum(
            "cqhd,ckhd->chqk", grad_out, value_block, preferred_element_type=jnp.float32
        )
        score_grad = (probs * (prob_grad - delta[..., None])).astype(jnp.bfloat16)
        query_grad = (
            query_grad
            + jnp.einsum(
                "chqk,ckhd->cqhd", score_grad, key_block, preferred_element_type=jnp.float32
            )
            * score_scale
        )
        key_part = (
            jnp.einsum("chqk,cqhd->ckhd", score_grad, queries, preferred_element_type=jnp.float32)
            * score_scale
        )
        flat_width = head_count * head_width
        key_grads = add_rows(
            key_grads, key_part.reshape(clip_count, block_rows, flat_width), offset
        )
        value_grads = add_rows(
            value_grads, value_part.reshape(clip_count, block_rows, flat_width), offset
        )
        return (query_grad, key_grads, value_grads)

    initial = (jnp.zeros(queries.shape, jnp.float32), key_grads, value_grads)
    return lax.fori_loop(0, key_frames, key_step, initial)


def shards(
    inputs,
    cotangent,
    context,
    levels,
    w_qkv,
    b_qkv,
    w_out,
    b_out,
    w_up,
    b_up,
    w_down,
    b_down,
    w_mod,
    b_mod,
):
    gathered = (
        lax.all_gather(w_qkv, ("dp", "seq"), axis=0, tiled=True),
        lax.all_gather(b_qkv, ("dp", "seq"), axis=0, tiled=True),
        lax.all_gather(w_out, ("dp", "seq"), axis=0, tiled=True),
        lax.all_gather(b_out, ("dp", "seq"), axis=0, tiled=True),
        lax.all_gather(w_up, ("dp", "seq"), axis=0, tiled=True),
        lax.all_gather(b_up, ("dp", "seq"), axis=0, tiled=True),
        lax.all_gather(w_down, ("dp", "seq"), axis=0, tiled=True),
        lax.all_gather(b_down, ("dp", "seq"), axis=0, tiled=True),
        lax.all_gather(w_mod, ("dp", "seq"), axis=0, tiled=True),
        lax.all_gather(b_mod, ("dp", "seq"), axis=0, tiled=True),
    )
    (
        qkv_weight,
        qkv_bias,
        out_weight,
        out_bias,
        up_weight,
        up_bias,
        down_weight,
        down_bias,
        mod_weight,
        mod_bias,
    ) = gathered
    own_frame = lax.axis_index("seq")
    clip_count = inputs.shape[0]
    patches = inputs.shape[1]
    row_count = clip_count * patches
    effective = jnp.where(own_frame < context, 0, levels[:, 0])
    condition = jax.nn.silu(level_embedding(effective, D)).astype(jnp.bfloat16)
    modulation = jnp.dot(
        condition, mod_weight, preferred_element_type=jnp.float32
    ) + mod_bias.astype(jnp.float32)
    shift_attend, scale_attend, gate_attend, shift_feed, scale_feed, gate_feed = jnp.split(
        modulation[:, None, :], 6, axis=-1
    )
    start_rows = inputs.astype(jnp.float32)
    normed, inv_std = layer_norm(start_rows)
    hidden = (
        (normed * (1.0 + scale_attend) + shift_attend).astype(jnp.bfloat16).reshape(row_count, D)
    )
    qkv_rows = jnp.dot(hidden, qkv_weight, preferred_element_type=jnp.float32) + qkv_bias.astype(
        jnp.float32
    )
    query_raw = qkv_rows[:, :D].reshape(clip_count, patches, H, HD)
    key_raw = qkv_rows[:, D : 2 * D].reshape(clip_count, patches, H, HD)
    value_raw = qkv_rows[:, 2 * D :].reshape(clip_count, patches, H, HD)
    patch_index = jnp.arange(patches)
    angles = rope_angles(jnp.full((patches,), own_frame), patch_index // PW, patch_index % PW, HD)
    cosine = jnp.cos(angles)
    sine_table = jnp.sin(angles)
    queries = rotate(query_raw, cosine, sine_table).astype(jnp.bfloat16)
    key_rows = rotate(key_raw, cosine, sine_table).astype(jnp.bfloat16)
    value_rows = value_raw.astype(jnp.bfloat16)
    key_send = key_rows.reshape(clip_count, patches, D)
    value_send = value_rows.reshape(clip_count, patches, D)
    all_keys, all_values = (
        lax.all_gather(key_send, "seq", axis=1, tiled=True),
        lax.all_gather(value_send, "seq", axis=1, tiled=True),
    )
    attended, log_total = attend_rows(queries, all_keys, all_values, own_frame + 1, patches)
    attended_low = attended.astype(jnp.bfloat16)
    attended_flat = attended_low.reshape(row_count, D)
    branch = (
        jnp.dot(attended_flat, out_weight, preferred_element_type=jnp.float32)
        + out_bias.astype(jnp.float32)
    ).reshape(clip_count, patches, D)
    middle = start_rows + gate_attend * branch
    normed_mid, inv_std_mid = layer_norm(middle)
    hidden_mid = (
        (normed_mid * (1.0 + scale_feed) + shift_feed).astype(jnp.bfloat16).reshape(row_count, D)
    )
    up_rows = jnp.dot(hidden_mid, up_weight, preferred_element_type=jnp.float32) + up_bias.astype(
        jnp.float32
    )
    activated = gelu_tanh(up_rows).astype(jnp.bfloat16)
    down_rows = (
        jnp.dot(activated, down_weight, preferred_element_type=jnp.float32)
        + down_bias.astype(jnp.float32)
    ).reshape(clip_count, patches, D)
    layer_out = middle + gate_feed * down_rows
    live_mask = (own_frame >= context).astype(jnp.float32)[:, None, None]
    out_grad = cotangent.astype(jnp.float32) * live_mask
    gate_feed_grad = jnp.sum(out_grad * down_rows, axis=1)
    down_grad = (out_grad * gate_feed).astype(jnp.bfloat16).reshape(row_count, D)
    g_wdown = outer_sum(activated, down_grad)
    g_bdown = jnp.sum(down_grad.astype(jnp.float32), axis=0)
    act_grad = back_dot(down_grad, down_weight)
    gelu_value, gelu_pull = jax.vjp(gelu_tanh, up_rows)
    up_grad = gelu_pull(act_grad)[0].astype(jnp.bfloat16)
    g_wup = outer_sum(hidden_mid, up_grad)
    g_bup = jnp.sum(up_grad.astype(jnp.float32), axis=0)
    hidden_mid_grad = back_dot(up_grad, up_weight).reshape(clip_count, patches, D)
    scale_feed_grad = jnp.sum(hidden_mid_grad * normed_mid, axis=1)
    shift_feed_grad = jnp.sum(hidden_mid_grad, axis=1)
    middle_grad = out_grad + norm_back(
        normed_mid, inv_std_mid, hidden_mid_grad * (1.0 + scale_feed)
    )
    gate_attend_grad = jnp.sum(middle_grad * branch, axis=1)
    branch_grad = (middle_grad * gate_attend).astype(jnp.bfloat16).reshape(row_count, D)
    g_wout = outer_sum(attended_flat, branch_grad)
    g_bout = jnp.sum(branch_grad.astype(jnp.float32), axis=0)
    attended_grad = (
        back_dot(branch_grad, out_weight).astype(jnp.bfloat16).reshape(clip_count, patches, H, HD)
    )
    zero_keys = jnp.zeros(all_keys.shape, jnp.float32)
    query_grad_rot, key_grad_all, value_grad_all = attend_back(
        queries,
        all_keys,
        all_values,
        attended_grad,
        attended,
        log_total,
        own_frame + 1,
        patches,
        zero_keys,
        zero_keys,
    )
    key_grad_sum, value_grad_sum = (
        lax.psum_scatter(
            key_grad_all.astype(jnp.bfloat16), "seq", scatter_dimension=1, tiled=True
        ).astype(jnp.float32),
        lax.psum_scatter(
            value_grad_all.astype(jnp.bfloat16), "seq", scatter_dimension=1, tiled=True
        ).astype(jnp.float32),
    )
    query_grad = unrotate(query_grad_rot, cosine, sine_table).astype(jnp.bfloat16)
    key_grad = unrotate(
        key_grad_sum.reshape(clip_count, patches, H, HD), cosine, sine_table
    ).astype(jnp.bfloat16)
    value_grad = value_grad_sum.astype(jnp.bfloat16)
    qkv_grad = jnp.concatenate(
        [
            query_grad.reshape(row_count, D),
            key_grad.reshape(row_count, D),
            value_grad.reshape(row_count, D),
        ],
        axis=-1,
    )
    g_wqkv = outer_sum(hidden, qkv_grad)
    g_bqkv = jnp.sum(qkv_grad.astype(jnp.float32), axis=0)
    hidden_grad = back_dot(qkv_grad, qkv_weight).reshape(clip_count, patches, D)
    scale_attend_grad = jnp.sum(hidden_grad * normed, axis=1)
    shift_attend_grad = jnp.sum(hidden_grad, axis=1)
    input_grad = middle_grad + norm_back(normed, inv_std, hidden_grad * (1.0 + scale_attend))
    mod_grad = jnp.concatenate(
        [
            shift_attend_grad,
            scale_attend_grad,
            gate_attend_grad,
            shift_feed_grad,
            scale_feed_grad,
            gate_feed_grad,
        ],
        axis=-1,
    ).astype(jnp.bfloat16)
    g_wmod = outer_sum(condition, mod_grad)
    g_bmod = jnp.sum(mod_grad.astype(jnp.float32), axis=0)
    summed = (
        lax.psum_scatter(g_wqkv, ("dp", "seq"), scatter_dimension=0, tiled=True),
        lax.psum_scatter(g_bqkv, ("dp", "seq"), scatter_dimension=0, tiled=True),
        lax.psum_scatter(g_wout, ("dp", "seq"), scatter_dimension=0, tiled=True),
        lax.psum_scatter(g_bout, ("dp", "seq"), scatter_dimension=0, tiled=True),
        lax.psum_scatter(g_wup, ("dp", "seq"), scatter_dimension=0, tiled=True),
        lax.psum_scatter(g_bup, ("dp", "seq"), scatter_dimension=0, tiled=True),
        lax.psum_scatter(g_wdown, ("dp", "seq"), scatter_dimension=0, tiled=True),
        lax.psum_scatter(g_bdown, ("dp", "seq"), scatter_dimension=0, tiled=True),
        lax.psum_scatter(g_wmod, ("dp", "seq"), scatter_dimension=0, tiled=True),
        lax.psum_scatter(g_bmod, ("dp", "seq"), scatter_dimension=0, tiled=True),
    )
    return (layer_out.astype(jnp.bfloat16), input_grad.astype(jnp.bfloat16)) + tuple(summed)


def solution(mesh):
    placed = (
        P("dp", "seq", None),
        P("dp", "seq", None),
        P("dp"),
        P("dp", "seq"),
        P(("dp", "seq"), None),
        P(("dp", "seq")),
        P(("dp", "seq"), None),
        P(("dp", "seq")),
        P(("dp", "seq"), None),
        P(("dp", "seq")),
        P(("dp", "seq"), None),
        P(("dp", "seq")),
        P(("dp", "seq"), None),
        P(("dp", "seq")),
    )
    return jax.shard_map(
        shards,
        mesh=mesh,
        in_specs=placed,
        out_specs=(
            P("dp", "seq", None),
            P("dp", "seq", None),
            P(("dp", "seq"), None),
            P(("dp", "seq")),
            P(("dp", "seq"), None),
            P(("dp", "seq")),
            P(("dp", "seq"), None),
            P(("dp", "seq")),
            P(("dp", "seq"), None),
            P(("dp", "seq")),
            P(("dp", "seq"), None),
            P(("dp", "seq")),
        ),
        check_vma=False,
    )
```

profile of v0, /device:TPU:0, one launch (start us, length us, event | category | flops | bytes accessed | tf_op | source)
XLA Modules:
  0.0 2136.4 jit_solution(13719029510559314075)
XLA Ops:
  14.1 43.2 %all-reduce.10 = (bf16[3072]{0:T(1024)(128)(2,1)S(1)}, bf16[6144]{0:T(1024)(128)(2,1)S(1)}, bf16[1024]{0:T(1024)(128)(2,1)S(1)}, bf16[1024]{0:T(1024)(128)(2,1)S(1)}) all-reduce(bf16[3072]{0:T(1024)(128)(2,1)S(1)} %dynamic-update-slice.1, bf16[6144]{0:T(1024)(128)(2,1)S(1)} %dynamic-update-slice, ...), channel_id=1, replica_groups=mesh['dp'=4,'seq'=8] {'dp','seq'}, use_global_device_ids=true, to_apply=%add.1 | all-reduce | flops 11264 | bytes 45056
  59.8 51.1 %all-gather.10.cloned.1.call-done = bf16[1024,6144]{1,0:T(8,128)(2,1)} async-done(((bf16[32,6144]{1,0:T(8,128)(2,1)}), bf16[1024,6144]{1,0:T(8,128)(2,1)}) %all-gather.10.cloned.1.call-update) | async-done | bytes 12582928 | tf_op jit(solution)/shard_map/all_gather | solution.py:237
  117.2 64.4 %all-gather.12.cloned.1.call-done = bf16[1024,3072]{1,0:T(8,128)(2,1)} async-done(((bf16[32,3072]{1,0:T(8,128)(2,1)}), bf16[1024,3072]{1,0:T(8,128)(2,1)}) %all-gather.12.cloned.1.call-update) | async-done | bytes 6291472 | tf_op jit(solution)/shard_map/all_gather | solution.py:229
  197.1 66.3 %all-gather.1 = bf16[32,1,128]{2,1,0:T(2,128)(2,1)S(1)} all-gather(bf16[1,1,128]{2,1,0:T(2,128)(2,1)S(1)} %bitcast.299), channel_id=1, replica_groups=mesh['dp'=4,'seq'=8] {'dp','seq'}, dimensions={0}, use_global_device_ids=true | all-gather | bytes 8448 | tf_op jit(solution)/shard_map/all_gather | solution.py:234
  270.0 67.0 %all-gather.14.cloned.1.call-done = bf16[1,2048,1024]{1,2,0:T(8,128)(2,1)} async-done(((bf16[1,256,1024]{1,2,0:T(8,128)(2,1)}), bf16[1,2048,1024]{1,2,0:T(8,128)(2,1)}) %all-gather.14.cloned.1.call-update) | async-done | bytes 4194320 | tf_op jit(solution)/shard_map/all_gather | solution.py:285
  341.1 53.5 %all-gather.16.cloned.1.call-done = bf16[1024,1024]{1,0:T(8,128)(2,1)} async-done(((bf16[32,1024]{1,0:T(8,128)(2,1)}), bf16[1024,1024]{1,0:T(8,128)(2,1)}) %all-gather.16.cloned.1.call-update) | async-done | bytes 2097168 | tf_op jit(solution)/shard_map/all_gather | solution.py:231
  399.2 74.5 %all-gather.18.cloned.1.call-done = bf16[1024,4096]{1,0:T(8,128)(2,1)} async-done(((bf16[32,4096]{1,0:T(8,128)(2,1)}), bf16[1024,4096]{1,0:T(8,128)(2,1)}) %all-gather.18.cloned.1.call-update) | async-done | bytes 8388624 | tf_op jit(solution)/shard_map/all_gather | solution.py:233
  473.7 8.1 convolution_add_fusion
  481.8 70.9 %all-gather.20.cloned.1.call-done = bf16[4096,1024]{1,0:T(8,128)(2,1)} async-done(((bf16[128,1024]{1,0:T(8,128)(2,1)}), bf16[4096,1024]{1,0:T(8,128)(2,1)}) %all-gather.20.cloned.1.call-update) | async-done | bytes 8388624 | tf_op jit(solution)/shard_map/all_gather | solution.py:235
  552.8 11.7 convert_reduce_fusion
  564.5 6.7 fusion.55
  589.1 9.9 while.29
  614.9 143.6 %reduce-scatter.8.cloned.1.call-done = bf16[1,256,1024]{1,2,0:T(8,128)(2,1)} async-done(((bf16[1,2048,1024]{1,2,0:T(8,128)(2,1)}), bf16[1,256,1024]{1,2,0:T(8,128)(2,1)}) %reduce-scatter.8.cloned.1.call-update) | async-done | bytes 524304 | tf_op jit(solution)/shard_map/reduce_scatter | solution.py:347
  760.1 90.7 %reduce-scatter.10.cloned.1.call-done = bf16[1,256,1024]{1,2,0:T(8,128)(2,1)} async-done(((bf16[1,2048,1024]{1,2,0:T(8,128)(2,1)}), bf16[1,256,1024]{1,2,0:T(8,128)(2,1)}) %reduce-scatter.10.cloned.1.call-update) | async-done | bytes 524304 | tf_op jit(solution)/shard_map/reduce_scatter | solution.py:350
  850.8 7.6 fusion.80
  859.5 10.8 fusion.66
  871.5 9.8 fusion.84
  888.6 11.6 broadcast_multiply_fusion
  902.0 41.7 %all-reduce.9 = (f32[3072]{0:T(1024)S(1)}, f32[1024]{0:T(1024)S(1)}, f32[4096]{0:T(1024)S(1)}, f32[1024]{0:T(1024)S(1)}, f32[6144]{0:T(1024)S(1)}) all-reduce(f32[3072]{0:T(1024)S(1)} %convert_reduce_fusion.1, f32[1024]{0:T(1024)S(1)} %get-tuple-element.241, ...), channel_id=6, replica_groups=mesh['dp'=4,'seq'=8] {'dp','seq'}, use_global_device_ids=true, to_apply=%region_19.20.clone | all-reduce | flops 15360 | bytes 110592
  949.2 47.6 %reduce-scatter.14.cloned.1.call-done = f32[32,1024]{1,0:T(8,128)} async-done(((f32[1024,1024]{1,0:T(8,128)}), f32[32,1024]{1,0:T(8,128)}) %reduce-scatter.14.cloned.1.call-update) | async-done | bytes 131088 | tf_op jit(solution)/shard_map/reduce_scatter | solution.py:389
  996.7 159.9 %reduce-scatter.12.cloned.1.call-done = f32[32,3072]{1,0:T(8,128)} async-done(((f32[1024,3072]{1,0:T(8,128)}), f32[32,3072]{1,0:T(8,128)}) %reduce-scatter.12.cloned.1.call-update) | async-done | bytes 393232 | tf_op jit(solution)/shard_map/reduce_scatter | solution.py:387
  1156.7 360.0 %reduce-scatter.18.cloned.1.call-done = f32[128,1024]{1,0:T(8,128)} async-done(((f32[4096,1024]{1,0:T(8,128)}), f32[128,1024]{1,0:T(8,128)}) %reduce-scatter.18.cloned.1.call-update) | async-done | bytes 524304 | tf_op jit(solution)/shard_map/reduce_scatter | solution.py:393
  1516.7 360.4 %reduce-scatter.16.cloned.1.call-done = f32[32,4096]{1,0:T(8,128)} async-done(((f32[1024,4096]{1,0:T(8,128)}), f32[32,4096]{1,0:T(8,128)}) %reduce-scatter.16.cloned.1.call-update) | async-done | bytes 524304 | tf_op jit(solution)/shard_map/reduce_scatter | solution.py:391
  1877.0 252.7 %reduce-scatter.20.cloned.1.call-done = f32[32,6144]{1,0:T(8,128)} async-done(((f32[1024,6144]{1,0:T(8,128)}), f32[32,6144]{1,0:T(8,128)}) %reduce-scatter.20.cloned.1.call-update) | async-done | bytes 786448 | tf_op jit(solution)/shard_map/reduce_scatter | solution.py:395
  (166 shorter events, 110.1 us)
Async XLA Ops:
  7.2 103.7 %all-gather.10.cloned.1.call-start = ((), (), s32[]{:S(2)}) async-start(), calls=%async_computation.7 | async-start | bytes 12976128 | tf_op jit(solution)/shard_map/all_gather | solution.py:237
  7.9 173.7 %all-gather.12.cloned.1.call-start = ((), (), s32[]{:S(2)}) async-start(), calls=%async_computation.8 | async-start | bytes 6488064 | tf_op jit(solution)/shard_map/all_gather | solution.py:229
  8.7 254.8 %all-gather.22.cloned.1.call-start = ((), (), s32[]{:S(2)}) async-start(), calls=%async_computation.20 | async-start | bytes 4718592 | tf_op jit(solution)/shard_map/all_gather | solution.py:286
  59.8 121.9 %copy-start = (bf16[1,256,1024]{2,1,0:T(8,128)(2,1)S(1)}, bf16[1,256,1024]{2,1,0:T(8,128)(2,1)}, u32[]{:S(2)}) copy-start(bf16[1,256,1024]{2,1,0:T(8,128)(2,1)} %param.18) | copy-start | bytes 1572868
  189.0 148.0 %all-gather.14.cloned.1.call-start = ((), (), s32[]{:S(2)}) async-start(), calls=%async_computation.9 | async-start | bytes 4718592 | tf_op jit(solution)/shard_map/all_gather | solution.py:285
  195.1 199.5 %all-gather.16.cloned.1.call-start = ((), (), s32[]{:S(2)}) async-start(), calls=%async_computation.10 | async-start | bytes 2162688 | tf_op jit(solution)/shard_map/all_gather | solution.py:231
  195.7 278.1 %all-gather.18.cloned.1.call-start = ((), (), s32[]{:S(2)}) async-start(), calls=%async_computation.11 | async-start | bytes 8650752 | tf_op jit(solution)/shard_map/all_gather | solution.py:233
  196.2 356.5 %all-gather.20.cloned.1.call-start = ((), (), s32[]{:S(2)}) async-start(), calls=%async_computation.12 | async-start | bytes 8650752 | tf_op jit(solution)/shard_map/all_gather | solution.py:235
  197.0 561.5 %reduce-scatter.8.cloned.1.call-start = ((), (), s32[]{:S(2)}) async-start(), calls=%async_computation.13 | async-start | bytes 4718592 | tf_op jit(solution)/shard_map/reduce_scatter | solution.py:347
  473.7 79.0 %copy-start.12 = (bf16[1,256,1024]{2,1,0:T(8,128)(2,1)S(1)}, bf16[1,256,1024]{2,1,0:T(8,128)(2,1)}, u32[]{:S(2)}) copy-start(bf16[1,256,1024]{2,1,0:T(8,128)(2,1)} %param.19) | copy-start | bytes 1572868
  552.8 11.7 copy-start.2
  564.4 6.8 copy-start.15
  564.4 7.0 copy-start.4
  564.4 7.0 copy-start.16
  564.5 8.1 copy-start.19
  572.5 5.0 copy-start.14
  605.1 245.7 %reduce-scatter.10.cloned.1.call-start = ((), (), s32[]{:S(2)}) async-start(), calls=%async_computation.14 | async-start | bytes 4718592 | tf_op jit(solution)/shard_map/reduce_scatter | solution.py:350
  611.1 385.6 %reduce-scatter.14.cloned.1.call-start = ((), (), s32[]{:S(2)}) async-start(), calls=%async_computation.16 | async-start | bytes 4325376 | tf_op jit(solution)/shard_map/reduce_scatter | solution.py:389
  614.8 541.9 %reduce-scatter.12.cloned.1.call-start = ((), (), s32[]{:S(2)}) async-start(), calls=%async_computation.15 | async-start | bytes 12976128 | tf_op jit(solution)/shard_map/reduce_scatter | solution.py:387
  858.4 658.2 %reduce-scatter.18.cloned.1.call-start = ((), (), s32[]{:S(2)}) async-start(), calls=%async_computation.18 | async-start | bytes 17301504 | tf_op jit(solution)/shard_map/reduce_scatter | solution.py:393
  870.3 1006.7 %reduce-scatter.16.cloned.1.call-start = ((), (), s32[]{:S(2)}) async-start(), calls=%async_computation.17 | async-start | bytes 17301504 | tf_op jit(solution)/shard_map/reduce_scatter | solution.py:391
  881.4 7.3 copy-start.17
  881.4 1248.4 %reduce-scatter.20.cloned.1.call-start = ((), (), s32[]{:S(2)}) async-start(), calls=%async_computation.19 | async-start | bytes 25952256 | tf_op jit(solution)/shard_map/reduce_scatter | solution.py:395
  900.2 46.5 %copy-start.6 = (f32[1,256,1024]{2,1,0:T(8,128)S(1)}, f32[1,256,1024]{2,1,0:T(8,128)}, u32[]{:S(2)}) copy-start(f32[1,256,1024]{2,1,0:T(8,128)} %copy-done.5) | copy-start | bytes 3145732
  (10 other events, 14.9 us)
Sparse Core Ops, SparseCore 0:
  11.0 99.8 all-gather.9
  113.9 67.7 all-gather.11
  189.1 72.0 all-gather.21
  263.6 73.3 all-gather.13
  339.8 54.7 all-gather.15
  397.4 76.2 all-gather.17
  476.7 75.9 all-gather.19
  605.2 153.2 reduce-scatter.7
  762.6 88.1 reduce-scatter.9
  853.5 143.1 reduce-scatter.13
  1003.3 153.2 reduce-scatter.11
  1159.5 357.1 reduce-scatter.17
  1519.7 357.3 reduce-scatter.15
  1885.0 244.6 reduce-scatter.19
where the time goes:
time: 2140 us
  waiting for transfers between devices  1800 us (84%)
  blocking collectives  151 us (7%)
  matrix products  87.8 us (4%)
  local copies, waits for them, and re-layouts  41.6 us (2%)
  other arithmetic  39.1 us (2%)
    reduce_scatter x1, waiting for transfers between devices, shards(): lax.psum_scatter(g_wup, ('dp', 'seq'), scatter_dimension=0, tiled=True)  360 us
    reduce_scatter x1, waiting for transfers between devices, shards(): lax.psum_scatter(g_wdown, ('dp', 'seq'), scatter_dimension=0, tiled=True)  360 us
    reduce_scatter x1, waiting for transfers between devices, shards(): lax.psum_scatter(g_wmod, ('dp', 'seq'), scatter_dimension=0, tiled=True)  253 us
    reduce_scatter x1, waiting for transfers between devices, shards(): lax.psum_scatter(g_wqkv, ('dp', 'seq'), scatter_dimension=0, tiled=True)  160 us
    reduce_scatter x1, waiting for transfers between devices, shards(): lax.psum_scatter(key_grad_all.astype(jnp.bfloat16), 'seq', scatter_dimens...  144 us
    reduce_scatter x1, waiting for transfers between devices, shards(): lax.psum_scatter(value_grad_all.astype(jnp.bfloat16), 'seq', scatter_dime...  90.7 us
    unnamed x2, blocking collectives  84.9 us
    all_gather x1, waiting for transfers between devices, shards(): lax.all_gather(w_up, ('dp', 'seq'), axis=0, tiled=True)  74.5 us
  transfers between devices with their start and end apart: 14, of which 13 were waited for; matrix products, arithmetic and copies ran while one was open for 5% of the time, Pallas kernels for 0%

commit v1 on v0

v1 whole, which is shorter than its diff:
```python
import math

import jax
import jax.numpy as jnp
from jax import lax
from jax.experimental import pallas as pl
from jax.experimental.pallas import tpu as pltpu
from jax.sharding import Mesh, PartitionSpec as P

D = 1024
H = 16
HD = 64
PW = 16
EPS = 1e-06

ALL = ("p", "c", "r", "q")
SEQ = ("r", "q")
bf16 = jnp.bfloat16
f32 = jnp.float32


def layer_norm(values):
    row_mean = jnp.mean(values, axis=-1, keepdims=True)
    centred = values - row_mean
    inv_std = lax.rsqrt(jnp.mean(centred * centred, axis=-1, keepdims=True) + EPS)
    return (centred * inv_std, inv_std)


def norm_back(normed, inv_std, normed_grad):
    first_mean = jnp.mean(normed_grad, axis=-1, keepdims=True)
    second_mean = jnp.mean(normed_grad * normed, axis=-1, keepdims=True)
    return inv_std * (normed_grad - first_mean - normed * second_mean)


def level_embedding(effective, width):
    half_width = width // 2
    frequency = jnp.exp(
        -math.log(10000.0) * jnp.arange(half_width).astype(f32) / half_width
    )
    angles = effective.astype(f32)[..., None] * frequency
    return jnp.concatenate([jnp.cos(angles), jnp.sin(angles)], axis=-1)


def rope_angles(frame_pos, row_pos, column_pos, head_width):
    pair_count = head_width // 2
    time_pairs = head_width // 8
    space_pairs = 3 * head_width // 16
    pair_index = jnp.arange(pair_count)
    axis_pick = jnp.where(
        pair_index < time_pairs, 0, jnp.where(pair_index < time_pairs + space_pairs, 1, 2)
    )
    local_rank = jnp.where(
        axis_pick == 0,
        pair_index,
        jnp.where(axis_pick == 1, pair_index - time_pairs, pair_index - time_pairs - space_pairs),
    )
    group_size = jnp.where(axis_pick == 0, time_pairs, space_pairs)
    frequency = jnp.exp(-math.log(10000.0) * local_rank.astype(f32) / group_size.astype(f32))
    position = jnp.where(
        axis_pick == 0,
        frame_pos[:, None],
        jnp.where(axis_pick == 1, row_pos[:, None], column_pos[:, None]),
    )
    return position.astype(f32) * frequency


def outer_sum(left, right):
    return lax.dot_general(
        left, right, (((0,), (0,)), ((), ())), preferred_element_type=f32
    )


def back_dot(grads, weight):
    return lax.dot_general(
        grads, weight, (((1,), (1,)), ((), ())), preferred_element_type=f32
    )


def nt(a, b):
    return lax.dot_general(a, b, (((1,), (1,)), ((), ())), preferred_element_type=f32)


def attend_kernel(block, heads, q_ref, k_ref, vt_ref, ot_ref, lse_ref):
    frame = pl.program_id(0)
    for h in range(heads):
        query = q_ref[h]

        def step(j, carry):
            top, total, acc = carry
            rows = pl.ds(pl.multiple_of(j * block, block), block)
            scores = nt(k_ref[h, rows, :], query)
            new_top = jnp.maximum(top, jnp.max(scores, axis=0, keepdims=True))
            shrink = jnp.exp(top - new_top)
            weights = jnp.exp(scores - new_top)
            total = total * shrink + jnp.sum(weights, axis=0, keepdims=True)
            acc = acc * shrink + jnp.dot(
                vt_ref[h, :, rows], weights.astype(bf16), preferred_element_type=f32
            )
            return new_top, total, acc

        top, total, acc = lax.fori_loop(
            0,
            frame + 1,
            step,
            (
                jnp.full((1, block), -1e30, f32),
                jnp.zeros((1, block), f32),
                jnp.zeros((HD, block), f32),
            ),
        )
        ot_ref[h] = acc / total
        lse_ref[h] = top + jnp.log(total)


def attend(queries, keys, values_t, block):
    heads, tokens, _ = queries.shape
    frames = tokens // block
    return pl.pallas_call(
        lambda *refs: attend_kernel(block, heads, *refs),
        grid=(frames,),
        in_specs=[
            pl.BlockSpec((heads, block, HD), lambda i: (0, i, 0)),
            pl.BlockSpec((heads, tokens, HD), lambda i: (0, 0, 0)),
            pl.BlockSpec((heads, HD, tokens), lambda i: (0, 0, 0)),
        ],
        out_specs=[
            pl.BlockSpec((heads, HD, block), lambda i: (0, 0, i)),
            pl.BlockSpec((heads, 1, block), lambda i: (0, 0, i)),
        ],
        out_shape=[
            jax.ShapeDtypeStruct((heads, HD, tokens), f32),
            jax.ShapeDtypeStruct((heads, 1, tokens), f32),
        ],
        compiler_params=pltpu.CompilerParams(vmem_limit_bytes=40 << 20),
    )(queries, keys, values_t)


def attend_back_kernel(
    block, heads, frames, q_ref, k_ref, kt_ref, v_ref, do_ref, ot_ref, lse_ref,
    dqt_ref, dk_ref, dv_ref, delta_ref,
):
    dqt_ref[...] = jnp.zeros_like(dqt_ref)
    for h in range(heads):
        for i in range(frames):
            rows = slice(i * block, (i + 1) * block)
            grad_t = jnp.transpose(do_ref[h, rows, :].astype(f32))
            delta_ref[h, :, rows] = jnp.sum(grad_t * ot_ref[h, :, rows], axis=0, keepdims=True)

    def key_step(j, _):
        keys_at = pl.ds(pl.multiple_of(j * block, block), block)
        for h in range(heads):
            key = k_ref[h, keys_at, :]
            key_t = kt_ref[h, :, keys_at]
            value = v_ref[h, keys_at, :]

            def query_step(i, carry):
                dk, dv = carry
                rows = pl.ds(pl.multiple_of(i * block, block), block)
                query = q_ref[h, rows, :]
                grad = do_ref[h, rows, :]
                probs = jnp.exp(nt(key, query) - lse_ref[h, :, rows])
                prob_grad = nt(value, grad)
                score_grad = (probs * (prob_grad - delta_ref[h, :, rows])).astype(bf16)
                dv = dv + jnp.dot(probs.astype(bf16), grad, preferred_element_type=f32)
                dk = dk + jnp.dot(score_grad, query, preferred_element_type=f32)
                dqt_ref[h, :, rows] += jnp.dot(key_t, score_grad, preferred_element_type=f32)
                return dk, dv

            zero = jnp.zeros((block, HD), f32)
            dk, dv = lax.fori_loop(j, frames, query_step, (zero, zero))
            dk_ref[h, keys_at, :] = dk
            dv_ref[h, keys_at, :] = dv
        return 0

    lax.fori_loop(0, frames, key_step, 0)


def attend_back(queries, keys, keys_t, values, grad, out_t, lse, block):
    heads, tokens, _ = queries.shape
    frames = tokens // block
    return pl.pallas_call(
        lambda *refs: attend_back_kernel(block, heads, frames, *refs),
        out_shape=[
            jax.ShapeDtypeStruct((heads, HD, tokens), f32),
            jax.ShapeDtypeStruct((heads, tokens, HD), f32),
            jax.ShapeDtypeStruct((heads, tokens, HD), f32),
        ],
        scratch_shapes=[pltpu.VMEM((heads, 1, tokens), f32)],
        compiler_params=pltpu.CompilerParams(vmem_limit_bytes=48 << 20),
    )(queries, keys, keys_t, values, grad, out_t, lse)


def swap(values, axis):
    return lax.ppermute(values, axis, [(0, 1), (1, 0)])


def pair_up(values, axis):
    other = swap(values, axis)
    first = lax.axis_index(axis) == 0
    return jnp.stack([jnp.where(first, values, other), jnp.where(first, other, values)])


def line_gather(values, axis, size):
    me = lax.axis_index(axis)
    whole = jnp.zeros((size,) + values.shape, values.dtype)
    whole = lax.dynamic_update_index_in_dim(whole, values, me, 0)
    up, down = values, values
    for step in range(1, size):
        up = lax.ppermute(up, axis, [(i, i + 1) for i in range(size - 1)])
        down = lax.ppermute(down, axis, [(i + 1, i) for i in range(size - 1)])
        low, high = jnp.maximum(me - step, 0), jnp.minimum(me + step, size - 1)
        whole = lax.dynamic_update_index_in_dim(
            whole, jnp.where(me >= step, up, whole[low]), low, 0
        )
        whole = lax.dynamic_update_index_in_dim(
            whole, jnp.where(me + step < size, down, whole[high]), high, 0
        )
    return whole


def line_scatter(parts, axis, size):
    me = lax.axis_index(axis)
    total = lax.dynamic_index_in_dim(parts, me, 0, keepdims=False).astype(f32)
    for shift in range(1, size):
        mine = lax.dynamic_index_in_dim(parts, (me + shift) % size, 0, keepdims=False)
        total = total + lax.ppermute(
            mine.astype(bf16), axis, [(i, (i + shift) % size) for i in range(size)]
        ).astype(f32)
    return total


def chip_scatter(parts, sizes):
    half = parts.shape[-1] // 2
    one, two = parts[..., :half], parts[..., half:]
    one = line_scatter(jnp.moveaxis(one, 2, 0), "q", sizes["q"]).astype(bf16)
    two = line_scatter(two, "p", sizes["p"]).astype(bf16)
    one = line_scatter(one, "p", sizes["p"])
    two = line_scatter(jnp.moveaxis(two, 1, 0), "q", sizes["q"])
    both = jnp.concatenate([one, two], axis=-1).astype(bf16)
    return line_scatter(both, "r", sizes["r"])


def make_shards(sizes):
    seq = sizes["r"] * sizes["q"]
    dp = sizes["p"] * sizes["c"]
    devices = seq * dp
    heads = H // seq
    wide = heads * HD

    def spread(values, axes):
        return lax.all_to_all(values, axes, 0, 0, tiled=True)

    def shards(
        inputs, cotangent, context, levels, w_qkv, b_qkv, w_out, b_out, w_up, b_up,
        w_down, b_down, w_mod, b_mod,
    ):
        own_frame = lax.axis_index(SEQ)
        core = lax.axis_index("c")
        patches = inputs.shape[1]
        tokens = seq * patches
        own_rows = w_mod.shape[0]

        effective = jnp.where(own_frame < context, 0, levels[:, 0])
        condition = jax.nn.silu(level_embedding(effective, D)).astype(bf16)
        biases = jnp.concatenate([b_qkv, b_out, b_up, b_down, b_mod])
        first = jnp.concatenate(
            [
                condition.reshape(devices, own_rows),
                jnp.broadcast_to(biases, (devices, biases.shape[0])),
            ],
            axis=1,
        )
        first = spread(first, ALL)
        pieces = first[:, :own_rows]
        at = own_rows
        full = []
        for bias in (b_qkv, b_out, b_up, b_down, b_mod):
            size = bias.shape[0]
            full.append(first[:, at : at + size].reshape(-1).astype(f32))
            at += size
        qkv_bias, out_bias, up_bias, down_bias, mod_bias = full
        mod_parts = jnp.dot(pieces, w_mod, preferred_element_type=f32)
        modulation = jnp.sum(spread(mod_parts.astype(bf16), ALL).astype(f32), axis=0) + mod_bias
        shift_attend, scale_attend, gate_attend, shift_feed, scale_feed, gate_feed = jnp.split(
            modulation[None, :], 6, axis=-1
        )
        frame_mod = spread(jnp.broadcast_to(modulation[None, : 2 * D], (seq, 2 * D)), SEQ)

        own_qkv = jnp.transpose(w_qkv.reshape(own_rows, 3, seq, wide), (2, 0, 1, 3))
        own_qkv = jnp.broadcast_to(
            own_qkv.reshape(1, seq, own_rows, 3 * wide), (dp, seq, own_rows, 3 * wide)
        ).reshape(devices, own_rows, 3 * wide)
        own_qkv = spread(own_qkv, ALL).reshape(D, 3 * wide)

        def whole(weight):
            return lax.all_gather(weight, ALL, axis=0, tiled=True)

        out_weight, up_weight, down_weight = whole(w_out), whole(w_up), whole(w_down)
        qkv_weight = whole(w_qkv)

        rows = inputs[0]
        split = patches // 2
        part_a = line_gather(rows[:split], "r", sizes["r"])
        part_b = pair_up(rows[split:], "q")
        part_a = jnp.moveaxis(pair_up(part_a, "q"), 0, 1)
        part_b = line_gather(part_b, "r", sizes["r"])
        clip = jnp.concatenate([part_a, part_b], axis=2).reshape(seq, patches, D)

        clip_normed, _ = layer_norm(clip.astype(f32))
        hidden_all = (
            clip_normed * (1.0 + frame_mod[:, None, D:]) + frame_mod[:, None, :D]
        ).astype(bf16).reshape(tokens, D)
        own_bias = lax.dynamic_index_in_dim(
            qkv_bias.reshape(3, seq, wide), own_frame, 1, keepdims=False
        ).reshape(3 * wide)
        qkv_rows = jnp.dot(hidden_all, own_qkv, preferred_element_type=f32) + own_bias
        qkv_rows = jnp.transpose(qkv_rows.reshape(tokens, 3, heads, HD), (1, 2, 0, 3))
        token = jnp.arange(tokens)
        patch = token % patches
        angles = rope_angles(token // patches, patch // PW, patch % PW, HD)
        cosine, sine = jnp.cos(angles), jnp.sin(angles)
        cosine = jnp.concatenate([cosine, cosine], axis=-1)
        sine = jnp.concatenate([-sine, sine], axis=-1)

        def turn(values, way):
            turned = jnp.concatenate([values[..., HD // 2 :], values[..., : HD // 2]], axis=-1)
            return values * cosine + way * turned * sine

        score_scale = 1.0 / math.sqrt(HD)
        queries = (turn(qkv_rows[0], 1.0).astype(bf16) * score_scale).astype(bf16)
        keys = turn(qkv_rows[1], 1.0).astype(bf16)
        values = qkv_rows[2].astype(bf16)
        out_t, lse = attend(queries, keys, jnp.transpose(values, (0, 2, 1)), patches)

        attended = jnp.transpose(out_t.astype(bf16), (2, 0, 1)).reshape(seq, patches, wide)
        attended = jnp.transpose(spread(attended, SEQ), (1, 0, 2)).reshape(patches, D)

        start_rows = rows.astype(f32)
        branch = jnp.dot(attended, out_weight, preferred_element_type=f32) + out_bias
        middle = start_rows + gate_attend * branch
        normed_mid, inv_std_mid = layer_norm(middle)
        hidden_mid = (normed_mid * (1.0 + scale_feed) + shift_feed).astype(bf16)
        up_rows = jnp.dot(hidden_mid, up_weight, preferred_element_type=f32) + up_bias
        gelu_value, gelu_pull = jax.vjp(lambda u: jax.nn.gelu(u, approximate=True), up_rows)
        activated = gelu_value.astype(bf16)
        down_rows = jnp.dot(activated, down_weight, preferred_element_type=f32) + down_bias
        layer_out = middle + gate_feed * down_rows

        live = (own_frame >= context).astype(f32)[:, None]
        out_grad = cotangent[0].astype(f32) * live
        gate_feed_grad = jnp.sum(out_grad * down_rows, axis=0)
        down_grad = (out_grad * gate_feed).astype(bf16)
        g_bdown = jnp.sum(down_grad.astype(f32), axis=0)
        up_grad = gelu_pull(back_dot(down_grad, down_weight))[0].astype(bf16)
        g_bup = jnp.sum(up_grad.astype(f32), axis=0)
        hidden_mid_grad = back_dot(up_grad, up_weight)
        scale_feed_grad = jnp.sum(hidden_mid_grad * normed_mid, axis=0)
        shift_feed_grad = jnp.sum(hidden_mid_grad, axis=0)
        middle_grad = out_grad + norm_back(
            normed_mid, inv_std_mid, hidden_mid_grad * (1.0 + scale_feed)
        )
        gate_attend_grad = jnp.sum(middle_grad * branch, axis=0)
        branch_grad = (middle_grad * gate_attend).astype(bf16)
        g_bout = jnp.sum(branch_grad.astype(f32), axis=0)
        attended_grad = back_dot(branch_grad, out_weight).astype(bf16)

        grad_heads = jnp.transpose(attended_grad.reshape(patches, seq, wide), (1, 0, 2))
        grad_heads = spread(grad_heads, SEQ).reshape(tokens, heads, HD)
        grad_heads = jnp.transpose(grad_heads, (1, 0, 2))
        dq_t, dk, dv = attend_back(
            queries, keys, jnp.transpose(keys, (0, 2, 1)), values, grad_heads, out_t, lse, patches
        )
        dq = turn(jnp.transpose(dq_t, (0, 2, 1)) * score_scale, -1.0).astype(bf16)
        dk = turn(dk, -1.0).astype(bf16)
        dqkv = jnp.transpose(jnp.stack([dq, dk, dv.astype(bf16)]), (2, 0, 1, 3)).reshape(
            tokens, 3 * wide
        )
        qkv_grad = spread(dqkv.reshape(seq, patches, 3 * wide), SEQ)
        qkv_grad = jnp.transpose(
            qkv_grad.reshape(seq, patches, 3, wide), (1, 2, 0, 3)
        ).reshape(patches, 3 * D)
        g_bqkv = jnp.sum(qkv_grad.astype(f32), axis=0)
        hidden_grad = back_dot(qkv_grad, qkv_weight)
        normed, inv_std = layer_norm(start_rows)
        scale_attend_grad = jnp.sum(hidden_grad * normed, axis=0)
        shift_attend_grad = jnp.sum(hidden_grad, axis=0)
        input_grad = middle_grad + norm_back(
            normed, inv_std, hidden_grad * (1.0 + scale_attend)
        )

        g_own = outer_sum(hidden_all, dqkv).astype(bf16).reshape(devices, own_rows, 3 * wide)
        g_own = spread(g_own, ALL).reshape(dp, seq, own_rows, 3, wide)
        g_wqkv = jnp.transpose(jnp.sum(g_own.astype(f32), axis=0), (1, 2, 0, 3)).reshape(
            own_rows, 3 * D
        )

        def halves(values):
            return values.reshape(patches, sizes["p"], 2, -1)

        def shared(left, right):
            parted = halves(left)
            mine = lax.dynamic_index_in_dim(parted, core, 2, keepdims=False)
            theirs = lax.dynamic_index_in_dim(parted, 1 - core, 2, keepdims=False)
            mine = mine.reshape(patches, -1)
            got_left = swap(theirs.reshape(patches, -1), "c")
            got_right = swap(right, "c")
            total = outer_sum(
                jnp.concatenate([mine, got_left]), jnp.concatenate([right, got_right])
            ).astype(bf16)
            total = total.reshape(sizes["p"], sizes["r"], sizes["q"], -1, right.shape[1])
            return chip_scatter(total, sizes)

        g_wdown = shared(activated, down_grad)
        g_wup = shared(hidden_mid, up_grad)
        g_wout = shared(attended, branch_grad)

        mod_grad = jnp.concatenate(
            [
                shift_attend_grad, scale_attend_grad, gate_attend_grad,
                shift_feed_grad, scale_feed_grad, gate_feed_grad,
            ]
        ).astype(bf16)
        last = jnp.concatenate(
            [jnp.broadcast_to(mod_grad, (devices, 6 * D))]
            + [g.astype(bf16).reshape(devices, -1) for g in (g_bqkv, g_bout, g_bup, g_bdown)],
            axis=1,
        )
        last = spread(last, ALL)
        all_mod = last[:, : 6 * D]
        g_wmod = outer_sum(pieces, all_mod)
        device = lax.axis_index(ALL)
        g_bmod = jnp.sum(
            lax.dynamic_index_in_dim(
                all_mod.reshape(devices, devices, -1), device, 1, keepdims=False
            ).astype(f32),
            axis=0,
        )
        bias_sums = jnp.sum(last[:, 6 * D :].astype(f32), axis=0)
        at = 0
        sums = []
        for bias in (b_qkv, b_out, b_up, b_down):
            sums.append(bias_sums[at : at + bias.shape[0]])
            at += bias.shape[0]
        return (
            layer_out[None].astype(bf16), input_grad[None].astype(bf16),
            g_wqkv, sums[0], g_wout, sums[1], g_wup, sums[2], g_wdown, sums[3], g_wmod, g_bmod,
        )

    return shards


def solution(mesh):
    dp, seq = mesh.shape["dp"], mesh.shape["seq"]
    sizes = {"p": dp // 2, "c": 2, "r": seq // 2, "q": 2}
    fine = Mesh(mesh.devices.reshape(dp // 2, 2, seq // 2, 2), ALL)
    rows = P(("p", "c"), SEQ, None)
    weight, bias = P(ALL, None), P(ALL)
    pairs = (weight, bias)
    return jax.shard_map(
        make_shards(sizes),
        mesh=fine,
        in_specs=(rows, rows, P(("p", "c")), P(("p", "c"), SEQ)) + pairs * 5,
        out_specs=(rows, rows) + pairs * 5,
        check_vma=False,
    )
```

time: 2140 us -> 635 us (0.30)
  waiting for transfers between devices: 1800 us -> 139 us
  blocking collectives: 151 us -> 0 us
  starting transfers between devices: 0.73 us -> 131 us
  local copies, waits for them, and re-layouts: 41.6 us -> 133 us
  Pallas kernels: 0 us -> 63.9 us
  other arithmetic: 39.1 us -> 80.2 us
  matrix products: 87.8 us -> 60.7 us
    reduce_scatter x7 -> x0, waiting for transfers between devices: 1410 us -> none  [the longest x1 360 us: shards(): lax.psum_scatter(g_wup, ('dp', 'seq'), scatter_dimension=0, tiled=True)]
    all_gather x7 -> x4, waiting for transfers between devices: 381 us -> 0.01 us  [whole(): return lax.all_gather(weight, ALL, axis=0, tiled=True)]
    ppermute x0 -> x41, waiting for transfers between devices: none -> 118 us  [the longest x21 74.7 us: line_scatter(): lax.ppermute(mine.astype(bf16), axis, [(i, (i + shift) % size) for i in r...]
    unnamed x2 -> x0, blocking collectives: 84.9 us -> none
    ppermute x0 -> x41, starting transfers between devices: none -> 76.1 us  [the longest x21 32 us: line_scatter(): lax.ppermute(mine.astype(bf16), axis, [(i, (i + shift) % size) for i in r...]
    all_gather x1 -> x0, blocking collectives: 66.3 us -> none  [shards(): lax.all_gather(b_up, ('dp', 'seq'), axis=0, tiled=True)]
    pallas_call x0 -> x2, Pallas kernels: none -> 63.9 us  [the longest x1 33.2 us: attend_back(): pl.pallas_call(lambda *refs: attend_back_kernel(block, heads, frames, *re...]
    all_to_all x0 -> x9, starting transfers between devices: none -> 54.8 us  [spread(): return lax.all_to_all(values, axes, 0, 0, tiled=True)]
  transfers between devices with their start and end apart: 14 -> 54, of which waited for: 13 -> 14; matrix products, arithmetic and copies ran while one was open for 5% -> 40% of each run, Pallas kernels for 0% -> 10%
where the time goes in v1:
time: 635 us; the launch traced here: 625 us
  waiting for transfers between devices  139 us (22%)
  local copies, waits for them, and re-layouts  133 us (21%)
  starting transfers between devices  131 us (21%)
  other arithmetic  80.2 us (13%)
  Pallas kernels  63.9 us (10%)
  matrix products  60.7 us (10%)
  between operations  17.1 us (3%)
    ppermute x21, waiting for transfers between devices, line_scatter(): lax.ppermute(mine.astype(bf16), axis, [(i, (i + shift) % size) for i in r...  74.7 us
    all_to_all x9, starting transfers between devices, spread(): return lax.all_to_all(values, axes, 0, 0, tiled=True)  54.8 us
    unnamed x153, local copies, waits for them, and re-layouts  43.6 us
    ppermute x6, waiting for transfers between devices, line_gather(): up = lax.ppermute(up, axis, [(i, i + 1) for i in range(size - 1)])  42.2 us
    pallas_call x1, Pallas kernels, attend_back(): pl.pallas_call(lambda *refs: attend_back_kernel(block, heads, frames, *re...  33.2 us
    ppermute x21, starting transfers between devices, line_scatter(): lax.ppermute(mine.astype(bf16), axis, [(i, (i + shift) % size) for i in r...  32 us
    ppermute x6, starting transfers between devices, line_gather(): up = lax.ppermute(up, axis, [(i, i + 1) for i in range(size - 1)])  31.4 us
    pallas_call x1, Pallas kernels, attend(): pl.pallas_call(lambda *refs: attend_kernel(block, heads, *refs), grid=(fr...  30.8 us
  transfers between devices with their start and end apart: 54, of which 14 were waited for; matrix products, arithmetic and copies ran while one was open for 40% of the time, Pallas kernels for 10%

profile of v1, /device:TPU:0, one launch (start us, length us, event | category | flops | bytes accessed | tf_op | source)
XLA Modules:
  0.0 624.9 jit_solution(7740392571923651696)
XLA Ops:
  12.5 5.7 collective-permute-start
  23.0 7.1 %all-to-all-start = ((bf16[32,2,256]{2,1,0:T(2,128)(2,1)}), bf16[32,2,256]{2,1,0:T(2,128)(2,1)}, u32[]{:S(2)}, u32[]{:S(2)}) async-start(bf16[32,2,256]{2,1,0:T(2,128)(2,1)} %reshape.628), calls=%async_computation | async-start | bytes 65536 | tf_op jit(solution)/shard_map/all_to_all | solution.py:251
  33.3 6.3 %fusion.61 = (f32[2048,32]{1,0:T(8,128)S(1)}, f32[2048,32]{1,0:T(8,128)}, f32[2048,32]{1,0:T(8,128)}) fusion(f32[32]{0:T(128)S(1)} %fusion.127, s32[2048]{0:T(1024)S(1)} %get-tuple-element.120, s32[2048]{0:T(1024)S(1)} %get-tuple-element.121, s32[2048]{0:T(1024)S(1)} %add_select_fusion.2, pred[32]{0:T(512)(128)(4,1)S(1)} %get-tuple-element.122, ...), kind=kLoop, calls=%fused_computation.135 | loop fusion | flops 327680 | bytes 811200 | tf_op jit(solution)/shard_map/cos | solution.py:321
  72.5 11.9 %collective-permute-done.2 = bf16[128,1024]{1,0:T(8,128)(2,1)S(1)} collective-permute-done((bf16[128,1024]{1,0:T(8,128)(2,1)}, bf16[128,1024]{1,0:T(8,128)(2,1)S(1)}, u32[]{:S(2)}, u32[]{:S(2)}) %collective-permute-start.2) | collective-permute-done | bytes 262176 | tf_op jit(solution)/shard_map/ppermute | solution.py:209
  84.4 7.4 %collective-permute-start.4 = (bf16[128,1024]{1,0:T(8,128)(2,1)S(1)}, bf16[128,1024]{1,0:T(8,128)(2,1)S(1)}, u32[]{:S(2)}, u32[]{:S(2)}) collective-permute-start(bf16[128,1024]{1,0:T(8,128)(2,1)S(1)} %collective-permute-done.2), channel_id=1, source_target_pairs={{0,2},{2,4},{4,6},{1,3},{3,5},{5,7},{8,10},{10,12},{12,14},{9,11},... | collective-permute-start | bytes 786440 | tf_op jit(solution)/shard_map/ppermute | solution.py:209
  96.7 5.8 collective-permute-start.10
  114.6 6.6 %all-to-all-start.2 = ((f32[8,1,2048]{2,1,0:T(1,128)}), f32[8,1,2048]{2,1,0:T(1,128)S(1)}, u32[]{:S(2)}, u32[]{:S(2)}) async-start(f32[8,1,2048]{2,1,0:T(1,128)} %broadcast_in_dim.196), calls=%async_computation.2 | async-start | bytes 131072 | tf_op jit(solution)/shard_map/all_to_all | solution.py:251
  124.0 7.3 %all-to-all-done.2 = f32[8,1,2048]{2,1,0:T(1,128)S(1)} async-done(((f32[8,1,2048]{2,1,0:T(1,128)}), f32[8,1,2048]{2,1,0:T(1,128)S(1)}, u32[]{:S(2)}, u32[]{:S(2)}) %all-to-all-start.2) | async-done | bytes 65568 | tf_op jit(solution)/shard_map/all_to_all | solution.py:251
  143.4 30.3 %collective-permute-done.12 = bf16[2,128,1024]{2,1,0:T(8,128)(2,1)S(1)} collective-permute-done((bf16[2,128,1024]{2,1,0:T(8,128)(2,1)}, bf16[2,128,1024]{2,1,0:T(8,128)(2,1)S(1)}, u32[]{:S(2)}, u32[]{:S(2)}) %collective-permute-start.12) | collective-permute-done | bytes 524320 | tf_op jit(solution)/shard_map/ppermute | solution.py:209
  186.9 5.9 convolution_add_fusion.1
  192.8 5.8 copy.88
  216.9 30.8 %shard_map.229 = (f32[2,64,2048]{2,1,0:T(8,128)S(1)}, f32[2,1,2048]{2,1,0:T(1,128)S(1)}) custom-call(bf16[2,2048,64]{2,1,0:T(8,128)(2,1)S(1)} %fusion.47.refs_0_, bf16[2,2048,64]{2,1,0:T(8,128)(2,1)S(1)} %fusion.18.refs_1_, bf16[2,64,2048]{2,1,0:T(8,128)(2,1)S(1)} %copy-done.4), custom_call_target="tpu_custom_call" | custom-call | tf_op jit(solution)/shard_map/pallas_call | solution.py:118
  249.8 15.7 %all-to-all-start.4 = ((bf16[8,256,128]{1,2,0:T(8,128)(2,1)}), bf16[8,256,128]{1,2,0:T(8,128)(2,1)}, u32[]{:S(2)}, u32[]{:S(2)}) async-start(bf16[8,256,128]{1,2,0:T(8,128)(2,1)} %copy.90), calls=%async_computation.4 | async-start | bytes 1048576 | tf_op jit(solution)/shard_map/all_to_all | solution.py:251
  269.1 11.2 %all-to-all-done.4 = bf16[8,256,128]{1,2,0:T(8,128)(2,1)} async-done(((bf16[8,256,128]{1,2,0:T(8,128)(2,1)}), bf16[8,256,128]{1,2,0:T(8,128)(2,1)}, u32[]{:S(2)}, u32[]{:S(2)}) %all-to-all-start.4) | async-done | bytes 524320 | tf_op jit(solution)/shard_map/all_to_all | solution.py:251
  297.6 9.5 %multiply_convert_fusion = (bf16[256,4096]{1,0:T(8,128)(2,1)}, f32[256,4096]{1,0:T(8,128)}) fusion(f32[4096]{0:T(1024)S(1)} %fusion.117, bf16[256,1024]{1,0:T(8,128)(2,1)} %add_convert_fusion.1, bf16[1024,4096]{1,0:T(8,128)(2,1)} %all-gather.7.cloned.1.call-done), kind=kOutput, calls=%fused_computation.23 | convolution fusion | flops 2157969408 | bytes 15220736 | tf_op jit(solution)/shard_map/dot_general | solution.py:343
  307.1 9.5 %fusion.134 = (bf16[4096]{0:T(1024)(128)(2,1)}, bf16[256,4096]{1,0:T(8,128)(2,1)}) fusion(f32[256,4096]{1,0:T(8,128)} %get-tuple-element.116, bf16[256,1024]{1,0:T(8,128)(2,1)} %get-tuple-element.31, bf16[4096,1024]{1,0:T(8,128)(2,1)} %all-gather.9.cloned.1.call-done), kind=kOutput, calls=%fused_computation.348 | convolution fusion | flops 2169499648 | bytes 15212544 | tf_op jit(solution)/shard_map/dot_general | solution.py:74
  347.8 6.3 %constant_dynamic-slice_fusion.3 = (bf16[256,2,1,1024]{3,2,1,0:T(2,128)(2,1)}, bf16[256,2,1,1024]{3,2,1,0:T(2,128)(2,1)}) fusion(bf16[256,2,2,1024]{3,2,1,0:T(2,128)(2,1)S(1)} %copy-done.9, s32[]{:T(128)S(6)} %select_n.472, s32[]{:T(128)S(6)} %select_n.473), kind=kLoop, calls=%fused_computation.256 | loop fusion | bytes 4194312 | tf_op jit(solution)/shard_map/jit(dynamic_index_in_dim)/dynamic_slice | solution.py:402
  354.7 5.8 copy.132
  360.5 5.8 copy.131
  388.0 33.2 %shard_map.230 = (f32[2,64,2048]{2,1,0:T(8,128)S(1)}, f32[2,2048,64]{2,1,0:T(8,128)}, f32[2,2048,64]{2,1,0:T(8,128)}) custom-call(bf16[2,2048,64]{2,1,0:T(8,128)(2,1)S(1)} %fusion.47.refs_0_, bf16[2,2048,64]{2,1,0:T(8,128)(2,1)S(1)} %fusion.18.refs_1_, bf16[2,64,2048]{2,1,0:T(8,128)(2,1)S(1)} %copy-done.5, ...), custom_call_target="tpu_custom_call" | custom-call | tf_op jit(solution)/shard_map/pallas_call | solution.py:181
  468.1 15.1 %collective-permute-done.34 = bf16[2,4,128,512]{3,2,1,0:T(8,128)(2,1)S(1)} collective-permute-done((bf16[2,4,128,512]{3,2,1,0:T(8,128)(2,1)S(1)}, bf16[2,4,128,512]{3,2,1,0:T(8,128)(2,1)S(1)}, u32[]{:S(2)}, u32[]{:S(2)}) %collective-permute-start.34) | collective-permute-done | bytes 1048608 | tf_op jit(solution)/shard_map/ppermute | solution.py:226
  503.6 10.1 %collective-permute-start.40 = (bf16[128,1024]{1,0:T(8,128)(2,1)}, bf16[128,1024]{1,0:T(8,128)(2,1)}, u32[]{:S(2)}, u32[]{:S(2)}) collective-permute-start(bf16[128,1024]{1,0:T(8,128)(2,1)} %get-tuple-element.67), channel_id=1, source_target_pairs={{0,6},{2,0},{4,2},{6,4},{1,7},{3,1},{5,3},{7,5},{8,14},{10,8},{12,... | collective-permute-start | bytes 786440 | tf_op jit(solution)/shard_map/ppermute | solution.py:226
  530.7 26.5 %collective-permute-done.39 = bf16[128,1024]{1,0:T(8,128)(2,1)} collective-permute-done((bf16[128,1024]{1,0:T(8,128)(2,1)}, bf16[128,1024]{1,0:T(8,128)(2,1)}, u32[]{:S(2)}, u32[]{:S(2)}) %collective-permute-start.39) | collective-permute-done | bytes 262176 | tf_op jit(solution)/shard_map/ppermute | solution.py:226
  595.6 14.5 %collective-permute-done.30 = bf16[32,4096]{1,0:T(8,128)(2,1)} collective-permute-done((bf16[32,4096]{1,0:T(8,128)(2,1)}, bf16[32,4096]{1,0:T(8,128)(2,1)}, u32[]{:S(2)}, u32[]{:S(2)}) %collective-permute-start.30) | collective-permute-done | bytes 262176 | tf_op jit(solution)/shard_map/ppermute | solution.py:226
  (429 shorter events, 313.9 us)
Async XLA Ops:
  7.3 274.8 %all-gather.5.cloned.1.call-start = ((), (), s32[]{:S(2)}) async-start(), calls=%async_computation.9 | async-start | bytes 2162688 | tf_op jit(solution)/shard_map/all_gather | solution.py:296
  8.0 289.6 %all-gather.7.cloned.1.call-start = ((), (), s32[]{:S(2)}) async-start(), calls=%async_computation.10 | async-start | bytes 8650752 | tf_op jit(solution)/shard_map/all_gather | solution.py:296
  8.8 298.4 %all-gather.9.cloned.1.call-start = ((), (), s32[]{:S(2)}) async-start(), calls=%async_computation.11 | async-start | bytes 8650752 | tf_op jit(solution)/shard_map/all_gather | solution.py:296
  12.5 49.2 %collective-permute-start = (bf16[128,1024]{1,0:T(8,128)(2,1)S(1)}, bf16[128,1024]{1,0:T(8,128)(2,1)}, u32[]{:S(2)}, u32[]{:S(2)}) collective-permute-start(bf16[128,1024]{1,0:T(8,128)(2,1)S(1)} %get-tuple-element.94), channel_id=1, source_target_pairs={{0,2},{2,4},{4,6},{1,3},{3,5},{5,7},{8,10},{10,12},{12,14},{9,11},... | collective-permute-start | bytes 786440 | tf_op jit(solution)/shard_map/ppermute | solution.py:209
  18.2 49.9 %collective-permute-start.1 = (bf16[128,1024]{1,0:T(8,128)(2,1)S(1)}, bf16[128,1024]{1,0:T(8,128)(2,1)}, u32[]{:S(2)}, u32[]{:S(2)}) collective-permute-start(bf16[128,1024]{1,0:T(8,128)(2,1)S(1)} %get-tuple-element.94), channel_id=1, source_target_pairs={{2,0},{4,2},{6,4},{3,1},{5,3},{7,5},{10,8},{12,10},{14,12},{11,9},... | collective-permute-start | bytes 786440 | tf_op jit(solution)/shard_map/ppermute | solution.py:210
  30.1 537.1 %all-gather.11.cloned.1.call-start = ((), (), s32[]{:S(2)}) async-start(), calls=%async_computation.12 | async-start | bytes 6488064 | tf_op jit(solution)/shard_map/all_gather | solution.py:296
  50.0 57.9 %all-to-all-start.1 = ((bf16[32,2,3072]{2,1,0:T(2,128)(2,1)}), bf16[32,2,3072]{2,1,0:T(2,128)(2,1)}, u32[]{:S(2)}, u32[]{:S(2)}) async-start(bf16[32,2,3072]{2,1,0:T(2,128)(2,1)} %reshape.630), calls=%async_computation.1 | async-start | bytes 786432 | tf_op jit(solution)/shard_map/all_to_all | solution.py:251
  122.0 51.9 %collective-permute-start.6 = (bf16[4,128,1024]{2,1,0:T(8,128)(2,1)}, bf16[4,128,1024]{2,1,0:T(8,128)(2,1)}, u32[]{:S(2)}, u32[]{:S(2)}) collective-permute-start(bf16[4,128,1024]{2,1,0:T(8,128)(2,1)} %bitcast_dynamic-update-slice_fusion.7), channel_id=1, source_target_pairs={{0,1},{1,0},{2,3},{3,2},{4,5},{5,4},{6,7},{7,6},{8,9},{9,8},{10,11... | collective-permute-start | bytes 3145736 | tf_op jit(solution)/shard_map/ppermute | solution.py:194
  132.3 54.6 %all-to-all-start.3 = ((bf16[32,32,384]{2,1,0:T(8,128)(2,1)}), bf16[32,32,384]{2,1,0:T(8,128)(2,1)}, u32[]{:S(2)}, u32[]{:S(2)}) async-start(bf16[32,32,384]{2,1,0:T(8,128)(2,1)} %bitcast.418), calls=%async_computation.3 | async-start | bytes 1572864 | tf_op jit(solution)/shard_map/all_to_all | solution.py:251
  268.0 178.6 %collective-permute-start.33 = (bf16[256,1024]{1,0:T(8,128)(2,1)}, bf16[256,1024]{1,0:T(8,128)(2,1)}, u32[]{:S(2)}, u32[]{:S(2)}) collective-permute-start(bf16[256,1024]{1,0:T(8,128)(2,1)} %get-tuple-element.31), channel_id=1, source_target_pairs={{0,8},{8,0},{1,9},{9,1},{2,10},{10,2},{3,11},{11,3},{4,12},{12,4},... | collective-permute-start | bytes 1572872 | tf_op jit(solution)/shard_map/ppermute | solution.py:194
  282.1 60.1 %collective-permute-start.14 = (bf16[256,512]{0,1:T(8,128)(2,1)}, bf16[256,512]{0,1:T(8,128)(2,1)}, u32[]{:S(2)}, u32[]{:S(2)}) collective-permute-start(bf16[256,512]{0,1:T(8,128)(2,1)} %bitcast.85), channel_id=1, source_target_pairs={{0,8},{8,0},{1,9},{9,1},{2,10},{10,2},{3,11},{11,3},{4,12},{12,4},... | collective-permute-start | bytes 786440 | tf_op jit(solution)/shard_map/ppermute | solution.py:194
  295.2 167.5 %collective-permute-start.23 = (bf16[256,512]{0,1:T(8,128)(2,1)}, bf16[256,512]{0,1:T(8,128)(2,1)}, u32[]{:S(2)}, u32[]{:S(2)}) collective-permute-start(bf16[256,512]{0,1:T(8,128)(2,1)} %bitcast.100), channel_id=1, source_target_pairs={{0,8},{8,0},{1,9},{9,1},{2,10},{10,2},{3,11},{11,3},{4,12},{12,4},... | collective-permute-start | bytes 786440 | tf_op jit(solution)/shard_map/ppermute | solution.py:194
  328.1 134.6 %collective-permute-start.24 = (bf16[256,4096]{1,0:T(8,128)(2,1)}, bf16[256,4096]{1,0:T(8,128)(2,1)}, u32[]{:S(2)}, u32[]{:S(2)}) collective-permute-start(bf16[256,4096]{1,0:T(8,128)(2,1)} %get-tuple-element.33), channel_id=1, source_target_pairs={{0,8},{8,0},{1,9},{9,1},{2,10},{10,2},{3,11},{11,3},{4,12},{12,4},... | collective-permute-start | bytes 6291464 | tf_op jit(solution)/shard_map/ppermute | solution.py:194
  360.5 87.9 %collective-permute-start.32 = (bf16[256,2048]{0,1:T(8,128)(2,1)}, bf16[256,2048]{0,1:T(8,128)(2,1)}, u32[]{:S(2)}, u32[]{:S(2)}) collective-permute-start(bf16[256,2048]{0,1:T(8,128)(2,1)} %bitcast.428), channel_id=1, source_target_pairs={{0,8},{8,0},{1,9},{9,1},{2,10},{10,2},{3,11},{11,3},{4,12},{12,4},... | collective-permute-start | bytes 3145736 | tf_op jit(solution)/shard_map/ppermute | solution.py:194
  376.2 76.7 %collective-permute-start.17 = (bf16[4,32,512]{2,1,0:T(8,128)(2,1)}, bf16[4,32,512]{2,1,0:T(8,128)(2,1)}, u32[]{:S(2)}, u32[]{:S(2)}) collective-permute-start(bf16[4,32,512]{2,1,0:T(8,128)(2,1)} %dynamic-slice_bitcast_fusion.8), channel_id=1, source_target_pairs={{0,16},{16,0},{1,17},{17,1},{2,18},{18,2},{3,19},{19,3},{4,20},{20... | collective-permute-start | bytes 393224 | tf_op jit(solution)/shard_map/ppermute | solution.py:226
  442.9 48.8 %all-to-all-start.7 = ((bf16[32,32,384]{2,1,0:T(8,128)(2,1)}), bf16[32,32,384]{2,1,0:T(8,128)(2,1)S(1)}, u32[]{:S(2)}, u32[]{:S(2)}) async-start(bf16[32,32,384]{2,1,0:T(8,128)(2,1)} %bitcast.77), calls=%async_computation.7 | async-start | bytes 1572864 | tf_op jit(solution)/shard_map/all_to_all | solution.py:251
  461.3 52.4 %collective-permute-start.22 = (bf16[32,1024]{1,0:T(8,128)(2,1)}, bf16[32,1024]{1,0:T(8,128)(2,1)}, u32[]{:S(2)}, u32[]{:S(2)}) collective-permute-start(bf16[32,1024]{1,0:T(8,128)(2,1)} %get-tuple-element.99), channel_id=1, source_target_pairs={{0,6},{2,0},{4,2},{6,4},{1,7},{3,1},{5,3},{7,5},{8,14},{10,8},{12,... | collective-permute-start | bytes 196616 | tf_op jit(solution)/shard_map/ppermute | solution.py:226
  462.7 51.0 %collective-permute-start.21 = (bf16[32,1024]{1,0:T(8,128)(2,1)S(1)}, bf16[32,1024]{1,0:T(8,128)(2,1)}, u32[]{:S(2)}, u32[]{:S(2)}) collective-permute-start(bf16[32,1024]{1,0:T(8,128)(2,1)S(1)} %get-tuple-element.98), channel_id=1, source_target_pairs={{0,4},{2,6},{4,0},{6,2},{1,5},{3,7},{5,1},{7,3},{8,12},{10,14},{12... | collective-permute-start | bytes 196616 | tf_op jit(solution)/shard_map/ppermute | solution.py:226
  462.7 53.8 %collective-permute-start.20 = (bf16[32,1024]{1,0:T(8,128)(2,1)S(1)}, bf16[32,1024]{1,0:T(8,128)(2,1)}, u32[]{:S(2)}, u32[]{:S(2)}) collective-permute-start(bf16[32,1024]{1,0:T(8,128)(2,1)S(1)} %get-tuple-element.97), channel_id=1, source_target_pairs={{0,2},{2,4},{4,6},{6,0},{1,3},{3,5},{5,7},{7,1},{8,10},{10,12},{12... | collective-permute-start | bytes 196616 | tf_op jit(solution)/shard_map/ppermute | solution.py:226
  492.5 73.4 %all-to-all-start.6 = ((bf16[8,256,384]{1,2,0:T(8,128)(2,1)}), bf16[8,256,384]{1,2,0:T(8,128)(2,1)S(1)}, u32[]{:S(2)}, u32[]{:S(2)}) async-start(bf16[8,256,384]{1,2,0:T(8,128)(2,1)} %copy.97), calls=%async_computation.6 | async-start | bytes 3145728 | tf_op jit(solution)/shard_map/all_to_all | solution.py:251
  498.0 61.2 %collective-permute-start.25 = (bf16[2,4,32,2048]{3,2,1,0:T(8,128)(2,1)}, bf16[2,4,32,2048]{3,2,1,0:T(8,128)(2,1)}, u32[]{:S(2)}, u32[]{:S(2)}) collective-permute-start(bf16[2,4,32,2048]{3,2,1,0:T(8,128)(2,1)} %dynamic-slice_bitcast_fusion.1), channel_id=1, source_target_pairs={{0,1},{1,0},{2,3},{3,2},{4,5},{5,4},{6,7},{7,6},{8,9},{9,8},{10,11... | collective-permute-start | bytes 3145736 | tf_op jit(solution)/shard_map/ppermute | solution.py:226
  513.7 43.5 %collective-permute-start.39 = (bf16[128,1024]{1,0:T(8,128)(2,1)}, bf16[128,1024]{1,0:T(8,128)(2,1)}, u32[]{:S(2)}, u32[]{:S(2)}) collective-permute-start(bf16[128,1024]{1,0:T(8,128)(2,1)} %get-tuple-element.66), channel_id=1, source_target_pairs={{0,4},{2,6},{4,0},{6,2},{1,5},{3,7},{5,1},{7,3},{8,12},{10,14},{12... | collective-permute-start | bytes 786440 | tf_op jit(solution)/shard_map/ppermute | solution.py:226
  513.7 43.5 %collective-permute-start.38 = (bf16[128,1024]{1,0:T(8,128)(2,1)}, bf16[128,1024]{1,0:T(8,128)(2,1)}, u32[]{:S(2)}, u32[]{:S(2)}) collective-permute-start(bf16[128,1024]{1,0:T(8,128)(2,1)} %get-tuple-element.65), channel_id=1, source_target_pairs={{0,2},{2,4},{4,6},{6,0},{1,3},{3,5},{5,7},{7,1},{8,10},{10,12},{12... | collective-permute-start | bytes 786440 | tf_op jit(solution)/shard_map/ppermute | solution.py:226
  516.5 45.1 %collective-permute-start.27 = (bf16[4,2,32,2048]{3,2,0,1:T(8,128)(2,1)}, bf16[4,2,32,2048]{3,2,0,1:T(8,128)(2,1)}, u32[]{:S(2)}, u32[]{:S(2)}) collective-permute-start(bf16[4,2,32,2048]{3,2,0,1:T(8,128)(2,1)} %bitcast.392), channel_id=1, source_target_pairs={{0,16},{16,0},{1,17},{17,1},{2,18},{18,2},{3,19},{19,3},{4,20},{20... | collective-permute-start | bytes 3145736 | tf_op jit(solution)/shard_map/ppermute | solution.py:226
  (94 other events, 1380.2 us)
Sparse Core Ops, SparseCore 0:
  11.1 63.0 all-gather.4
  77.1 109.8 all-gather.6
  190.1 76.3 all-gather.8
  269.3 68.1 all-gather.10

commit v2 on v1

v2 whole, which is shorter than its diff:
```python
import math

import jax
import jax.numpy as jnp
from jax import lax
from jax.experimental import pallas as pl
from jax.experimental.pallas import tpu as pltpu
from jax.sharding import Mesh, PartitionSpec as P

D = 1024
H = 16
HD = 64
PW = 16
EPS = 1e-06

ALL = ("p", "c", "r", "q")
SEQ = ("r", "q")
bf16 = jnp.bfloat16
SHORT = pl.CostEstimate(flops=1, bytes_accessed=1, transcendentals=0)
f32 = jnp.float32


def layer_norm(values):
    row_mean = jnp.mean(values, axis=-1, keepdims=True)
    centred = values - row_mean
    inv_std = lax.rsqrt(jnp.mean(centred * centred, axis=-1, keepdims=True) + EPS)
    return (centred * inv_std, inv_std)


def norm_back(normed, inv_std, normed_grad):
    first_mean = jnp.mean(normed_grad, axis=-1, keepdims=True)
    second_mean = jnp.mean(normed_grad * normed, axis=-1, keepdims=True)
    return inv_std * (normed_grad - first_mean - normed * second_mean)


def level_embedding(effective, width):
    half_width = width // 2
    frequency = jnp.exp(
        -math.log(10000.0) * jnp.arange(half_width).astype(f32) / half_width
    )
    angles = effective.astype(f32)[..., None] * frequency
    return jnp.concatenate([jnp.cos(angles), jnp.sin(angles)], axis=-1)


def rope_angles(frame_pos, row_pos, column_pos, head_width):
    pair_count = head_width // 2
    time_pairs = head_width // 8
    space_pairs = 3 * head_width // 16
    pair_index = jnp.arange(pair_count)
    axis_pick = jnp.where(
        pair_index < time_pairs, 0, jnp.where(pair_index < time_pairs + space_pairs, 1, 2)
    )
    local_rank = jnp.where(
        axis_pick == 0,
        pair_index,
        jnp.where(axis_pick == 1, pair_index - time_pairs, pair_index - time_pairs - space_pairs),
    )
    group_size = jnp.where(axis_pick == 0, time_pairs, space_pairs)
    frequency = jnp.exp(-math.log(10000.0) * local_rank.astype(f32) / group_size.astype(f32))
    position = jnp.where(
        axis_pick == 0,
        frame_pos[:, None],
        jnp.where(axis_pick == 1, row_pos[:, None], column_pos[:, None]),
    )
    return position.astype(f32) * frequency


def outer_sum(left, right):
    return lax.dot_general(
        left, right, (((0,), (0,)), ((), ())), preferred_element_type=f32
    )


def back_dot(grads, weight):
    return lax.dot_general(
        grads, weight, (((1,), (1,)), ((), ())), preferred_element_type=f32
    )


def nt(a, b):
    return lax.dot_general(a, b, (((1,), (1,)), ((), ())), preferred_element_type=f32)


def dot(a, b):
    return jnp.dot(a, b, preferred_element_type=f32)


def full_block(shape):
    return pl.BlockSpec(shape, lambda *_: (0,) * len(shape))


def project_kernel(
    heads, rows_ref, mod_ref, weight_ref, bias_ref, cos_ref, sin_ref,
    hidden_ref, q_ref, k_ref, kt_ref, v_ref, vt_ref,
):
    normed, _ = layer_norm(rows_ref[0].astype(f32))
    hidden = (normed * (1.0 + mod_ref[0, 1:2, :]) + mod_ref[0, 0:1, :]).astype(bf16)
    hidden_ref[...] = hidden
    made = dot(hidden, weight_ref[...]) + bias_ref[...]
    wide = heads * HD
    cosine, sine = cos_ref[...], sin_ref[...]

    def turn(values):
        half = HD // 2
        turned = jnp.concatenate([values[:, half:], values[:, :half]], axis=1)
        return values * cosine + turned * sine

    for h in range(heads):
        at = h * HD
        query = turn(made[:, at : at + HD]).astype(bf16).astype(f32)
        key = turn(made[:, wide + at : wide + at + HD])
        value = made[:, 2 * wide + at : 2 * wide + at + HD]
        q_ref[h] = (query * (1.0 / math.sqrt(HD))).astype(bf16)
        k_ref[h] = key.astype(bf16)
        kt_ref[h] = jnp.transpose(key).astype(bf16)
        v_ref[h] = value.astype(bf16)
        vt_ref[h] = jnp.transpose(value).astype(bf16)


def project(clip, frame_mod, weight, bias, cosine, sine, heads):
    frames, block, _ = clip.shape
    tokens = frames * block
    wide = heads * HD
    tall = pl.BlockSpec((heads, block, HD), lambda i: (0, i, 0))
    flat = pl.BlockSpec((heads, HD, block), lambda i: (0, 0, i))
    tall_shape = jax.ShapeDtypeStruct((heads, tokens, HD), bf16)
    flat_shape = jax.ShapeDtypeStruct((heads, HD, tokens), bf16)
    return pl.pallas_call(
        lambda *refs: project_kernel(heads, *refs),
        grid=(frames,),
        in_specs=[
            pl.BlockSpec((1, block, D), lambda i: (i, 0, 0)),
            pl.BlockSpec((1, 2, D), lambda i: (i, 0, 0)),
            full_block((D, 3 * wide)),
            full_block((1, 3 * wide)),
            pl.BlockSpec((block, HD), lambda i: (i, 0)),
            pl.BlockSpec((block, HD), lambda i: (i, 0)),
        ],
        out_specs=[pl.BlockSpec((block, D), lambda i: (i, 0)), tall, tall, flat, tall, flat],
        out_shape=[
            jax.ShapeDtypeStruct((tokens, D), bf16),
            tall_shape, tall_shape, flat_shape, tall_shape, flat_shape,
        ],
        compiler_params=pltpu.CompilerParams(vmem_limit_bytes=40 << 20),
        cost_estimate=SHORT,
    )(clip, frame_mod, weight, bias, cosine, sine)


def attend_kernel(
    block, heads, frames, q_ref, k_ref, vt_ref, ot_ref, out_ref, lse_ref, score_ref
):
    count = frames + 1

    def pair_step(first, _):
        second = frames - 1 - first

        def place(n):
            early = n <= first
            query_frame = jnp.where(early, first, second)
            key_frame = jnp.where(early, n, n - first - 1)
            return (
                early,
                pl.ds(pl.multiple_of(query_frame * block, block), block),
                pl.ds(pl.multiple_of(key_frame * block, block), block),
            )

        for h in range(heads):
            tops = []
            for n in range(count):
                _, rows, keys = place(n)
                scores = nt(k_ref[h, keys, :], q_ref[h, rows, :])
                score_ref[h, n] = scores
                tops.append(jnp.max(scores, axis=0, keepdims=True))
            low = jnp.full((1, block), -1e30, f32)
            top_a, top_b = low, low
            for n in range(count):
                early = n <= first
                top_a = jnp.maximum(top_a, jnp.where(early, tops[n], low))
                top_b = jnp.maximum(top_b, jnp.where(early, low, tops[n]))
            zero = jnp.zeros((1, block), f32)
            sum_a, sum_b = zero, zero
            acc_a = jnp.zeros((HD, block), f32)
            acc_b = acc_a
            for n in range(count):
                early, _, keys = place(n)
                weights = jnp.exp(score_ref[h, n] - jnp.where(early, top_a, top_b))
                part_sum = jnp.sum(weights, axis=0, keepdims=True)
                part = dot(vt_ref[h, :, keys], weights.astype(bf16))
                if n == 0:
                    sum_a, acc_a = part_sum, part
                elif n > (frames - 1) // 2:
                    sum_b, acc_b = sum_b + part_sum, acc_b + part
                else:
                    sum_a = sum_a + jnp.where(early, part_sum, 0.0)
                    sum_b = sum_b + jnp.where(early, 0.0, part_sum)
                    acc_a = acc_a + jnp.where(early, part, 0.0)
                    acc_b = acc_b + jnp.where(early, 0.0, part)
            for frame, top, total, acc in (
                (first, top_a, sum_a, acc_a), (second, top_b, sum_b, acc_b),
            ):
                rows = pl.ds(pl.multiple_of(frame * block, block), block)
                done = acc / total
                ot_ref[h, :, rows] = done
                out_ref[frame, :, h * HD : (h + 1) * HD] = jnp.transpose(done).astype(bf16)
                lse_ref[h, :, rows] = top + jnp.log(total)
        return 0

    lax.fori_loop(0, frames // 2, pair_step, 0)


def attend(queries, keys, values_t, block):
    heads, tokens, _ = queries.shape
    frames = tokens // block
    return pl.pallas_call(
        lambda *refs: attend_kernel(block, heads, frames, *refs),
        out_shape=[
            jax.ShapeDtypeStruct((heads, HD, tokens), f32),
            jax.ShapeDtypeStruct((frames, block, heads * HD), bf16),
            jax.ShapeDtypeStruct((heads, 1, tokens), f32),
        ],
        scratch_shapes=[pltpu.VMEM((heads, frames + 1, block, block), f32)],
        compiler_params=pltpu.CompilerParams(vmem_limit_bytes=40 << 20),
        cost_estimate=SHORT,
    )(queries, keys, values_t)


def attend_back_kernel(
    block, heads, frames, q_ref, k_ref, kt_ref, v_ref, do_ref, ot_ref, lse_ref, cos_ref, sin_ref,
    out_ref, dqt_ref, delta_ref,
):
    dqt_ref[...] = jnp.zeros_like(dqt_ref)
    wide = heads * HD
    scale = 1.0 / math.sqrt(HD)
    for i in range(frames):
        rows = slice(i * block, (i + 1) * block)
        for h in range(heads):
            grad_t = jnp.transpose(do_ref[i, :, h * HD : (h + 1) * HD].astype(f32))
            delta_ref[h, :, rows] = jnp.sum(grad_t * ot_ref[h, :, rows], axis=0, keepdims=True)

    def back(values, rows):
        half = HD // 2
        turned = jnp.concatenate([values[:, half:], values[:, :half]], axis=1)
        return (values * cos_ref[rows, :] - turned * sin_ref[rows, :]).astype(bf16)

    def pair_step(first, _):
        second = frames - 1 - first
        for h in range(heads):
            zero = jnp.zeros((block, HD), f32)
            dk_a, dv_a, dk_b, dv_b = zero, zero, zero, zero
            for n in range(frames + 1):
                early = n < frames - first
                query_frame = jnp.where(early, first + n, n - 1)
                key_frame = jnp.where(early, first, second)
                rows = pl.ds(pl.multiple_of(query_frame * block, block), block)
                keys = pl.ds(pl.multiple_of(key_frame * block, block), block)
                query = q_ref[h, rows, :]
                grad = do_ref[query_frame, :, h * HD : (h + 1) * HD]
                probs = jnp.exp(nt(k_ref[h, keys, :], query) - lse_ref[h, :, rows])
                prob_grad = nt(v_ref[h, keys, :], grad)
                score_grad = (probs * (prob_grad - delta_ref[h, :, rows])).astype(bf16)
                dv = dot(probs.astype(bf16), grad)
                dk = dot(score_grad, query)
                dqt_ref[h, :, rows] += dot(kt_ref[h, :, keys], score_grad)
                if n < frames - (frames - 1) // 2:
                    dk_a, dv_a = dk_a + dk, dv_a + dv
                elif n == frames:
                    dk_b, dv_b = dk_b + dk, dv_b + dv
                else:
                    dk_a = dk_a + jnp.where(early, dk, 0.0)
                    dv_a = dv_a + jnp.where(early, dv, 0.0)
                    dk_b = dk_b + jnp.where(early, 0.0, dk)
                    dv_b = dv_b + jnp.where(early, 0.0, dv)
            for frame, dk, dv in ((first, dk_a, dv_a), (second, dk_b, dv_b)):
                rows = pl.ds(pl.multiple_of(frame * block, block), block)
                at = wide + h * HD
                out_ref[frame, :, at : at + HD] = back(dk, rows)
                out_ref[frame, :, wide + at : wide + at + HD] = dv.astype(bf16)
        return 0

    lax.fori_loop(0, frames // 2, pair_step, 0)
    for i in range(frames):
        rows = slice(i * block, (i + 1) * block)
        for h in range(heads):
            out_ref[i, :, h * HD : (h + 1) * HD] = back(
                jnp.transpose(dqt_ref[h, :, rows]) * scale, rows
            )


def attend_back(queries, keys, keys_t, values, grad, out_t, lse, cosine, sine, block):
    heads, tokens, _ = queries.shape
    frames = tokens // block
    return pl.pallas_call(
        lambda *refs: attend_back_kernel(block, heads, frames, *refs),
        out_shape=jax.ShapeDtypeStruct((frames, block, 3 * heads * HD), bf16),
        scratch_shapes=[
            pltpu.VMEM((heads, HD, tokens), f32),
            pltpu.VMEM((heads, 1, tokens), f32),
        ],
        compiler_params=pltpu.CompilerParams(vmem_limit_bytes=48 << 20),
        cost_estimate=SHORT,
    )(queries, keys, keys_t, values, grad, out_t, lse, cosine, sine)


def middle_kernel(
    parts, tiles, att_ref, in_ref, cot_ref, mod_ref, live_ref, out_bias_ref, down_bias_ref,
    up_bias_ref, w_out_ref, w_up_ref, w_down_ref,
    layer_ref, grad_ref, act_ref, up_grad_ref, two_grad_ref, half_ref,
    att_grad_ref, stat_ref, g_bup_ref,
    att_all, branch_ref, middle_ref, normed_ref, inv_ref, hidden_ref, down_acc, back_acc,
):
    tile = pl.program_id(0)
    gate_a, shift_f, scale_f, gate_f = (mod_ref[i : i + 1, :] for i in (2, 3, 4, 5))
    groups, _, wide = att_ref.shape
    span = D // (2 * parts)

    def flat(ref):
        last = ref.shape[-1]
        return jnp.concatenate(
            [ref[:, p].reshape(-1, last) for p in range(ref.shape[1])], axis=0
        )

    def halves(start, values):
        for p in range(parts):
            for c in range(2):
                at = (2 * p + c) * span
                to = start + p * span
                half_ref[c, :, to : to + span] = values[:, at : at + span]

    @pl.when(tile == 0)
    def _():
        for g in range(groups):
            att_all[:, g * wide : (g + 1) * wide] = att_ref[g]
        attended = att_all[...]
        halves(D // 2, attended)
        branch = dot(attended, flat(w_out_ref)) + out_bias_ref[...]
        branch_ref[...] = branch
        middle = in_ref[...].astype(f32) + gate_a * branch
        middle_ref[...] = middle
        normed, inv_std = layer_norm(middle)
        normed_ref[...] = normed
        inv_ref[...] = inv_std
        hidden = (normed * (1.0 + scale_f) + shift_f).astype(bf16)
        hidden_ref[...] = hidden
        halves(0, hidden)
        two_grad_ref[0] = (cot_ref[...].astype(f32) * live_ref[...] * gate_f).astype(bf16)

    hidden = hidden_ref[...]
    down_grad = two_grad_ref[0]
    w_up, w_down = flat(w_up_ref), flat(w_down_ref)
    u = dot(hidden, w_up) + up_bias_ref[...]
    scale = math.sqrt(2.0 / math.pi)
    square = u * u
    bend = jnp.tanh(scale * (u + 0.044715 * (u * square)))
    rise = 0.5 * (1.0 + bend)
    slope = rise + (0.5 * scale) * u * (1.0 - bend * bend) * (1.0 + (3.0 * 0.044715) * square)
    act = (u * rise).astype(bf16)
    act_ref[0] = act
    down_part = dot(act, w_down)
    up_grad = (nt(down_grad, w_down) * slope).astype(bf16)
    up_grad_ref[...] = up_grad
    g_bup_ref[...] = jnp.sum(up_grad.astype(f32), axis=0, keepdims=True)
    back_part = nt(up_grad, w_up)

    @pl.when(tile == 0)
    def _():
        down_acc[...] = down_part
        back_acc[...] = back_part

    @pl.when(tile > 0)
    def _():
        down_acc[...] += down_part
        back_acc[...] += back_part

    @pl.when(tile == tiles - 1)
    def _():
        def put(at, values):
            stat_ref[at : at + 1, :] = jnp.sum(values, axis=0, keepdims=True)

        out_grad = cot_ref[...].astype(f32) * live_ref[...]
        down_rows = down_acc[...] + down_bias_ref[...]
        layer_ref[...] = (middle_ref[...] + gate_f * down_rows).astype(bf16)
        put(3, out_grad * down_rows)
        put(4, down_grad.astype(f32))
        hidden_grad = back_acc[...]
        normed = normed_ref[...]
        put(1, hidden_grad)
        put(2, hidden_grad * normed)
        middle_grad = out_grad + norm_back(normed, inv_ref[...], hidden_grad * (1.0 + scale_f))
        grad_ref[...] = middle_grad
        put(0, middle_grad * branch_ref[...])
        branch_grad = (middle_grad * gate_a).astype(bf16)
        two_grad_ref[1] = branch_grad
        put(5, branch_grad.astype(f32))
        put(6, jnp.zeros_like(out_grad))
        put(7, jnp.zeros_like(out_grad))
        att_grad = nt(branch_grad, flat(w_out_ref)).astype(bf16)
        for g in range(groups):
            att_grad_ref[g] = att_grad[:, g * wide : (g + 1) * wide]


def middle(attended, rows, cot, mod, live, biases, stack, parts):
    groups, patches, wide = attended.shape
    hidden_units = biases[2].shape[1]
    devices = stack.shape[0] * parts
    down_rows, up_rows = hidden_units // devices, D // devices
    first_up, first_out = down_rows // up_rows, (down_rows + up_rows * (hidden_units // D)) // up_rows
    span = hidden_units // (2 * parts)
    width = min(512, span)
    tiles = hidden_units // width
    tiles_part = tiles // parts
    per_span = span // width

    def half_at(t):
        block = t // per_span
        return (block % 2, 0, (block // 2) * per_span + t % per_span)

    token_shape = (patches, D)

    def shape(dims, dtype):
        return jax.ShapeDtypeStruct(dims, dtype)

    return pl.pallas_call(
        lambda *refs: middle_kernel(parts, tiles, *refs),
        grid=(tiles,),
        in_specs=[
            full_block(attended.shape), full_block(token_shape), full_block(token_shape),
            full_block((6, D)), full_block((1, 1)), full_block((1, D)), full_block((1, D)),
            pl.BlockSpec((1, width), lambda t: (0, t)),
            pl.BlockSpec((devices // parts, parts, up_rows, D), lambda t: (0, 0, first_out, 0)),
            pl.BlockSpec(
                (devices // parts, parts, up_rows, width),
                lambda t: (0, 0, first_up + t * width // D, t % (D // width)),
            ),
            pl.BlockSpec(
                (width // down_rows, 1, down_rows, D),
                lambda t: (t % tiles_part, t // tiles_part, 0, 0),
            ),
        ],
        out_specs=[
            full_block(token_shape), full_block(token_shape),
            pl.BlockSpec((1, patches, width), half_at),
            pl.BlockSpec((patches, width), lambda t: (0, t)),
            full_block((2,) + token_shape), full_block((2,) + token_shape),
            full_block(attended.shape), full_block((8, D)),
            pl.BlockSpec((1, width), lambda t: (0, t)),
        ],
        out_shape=[
            shape(token_shape, bf16), shape(token_shape, f32),
            shape((2, patches, hidden_units // 2), bf16), shape((patches, hidden_units), bf16),
            shape((2,) + token_shape, bf16), shape((2,) + token_shape, bf16),
            shape(attended.shape, bf16), shape((8, D), f32),
            shape((1, hidden_units), f32),
        ],
        scratch_shapes=[
            pltpu.VMEM(token_shape, bf16), pltpu.VMEM(token_shape, f32),
            pltpu.VMEM(token_shape, f32), pltpu.VMEM(token_shape, f32),
            pltpu.VMEM((patches, 1), f32), pltpu.VMEM(token_shape, bf16),
            pltpu.VMEM(token_shape, f32), pltpu.VMEM(token_shape, f32),
        ],
        compiler_params=pltpu.CompilerParams(vmem_limit_bytes=56 << 20),
        cost_estimate=SHORT,
    )(attended, rows, cot, mod, live, *biases, stack, stack, stack)


def swap(values, axis):
    return lax.ppermute(values, axis, [(0, 1), (1, 0)])


def shifts(values, axis, size):
    me = lax.axis_index(axis)
    found = [(me, values)]
    for shift in range(1, size):
        pairs = [(i, (i + shift) % size) for i in range(size)]
        found.append(((me + size - shift) % size, lax.ppermute(values, axis, pairs)))
    return found


def line_gather(values, axis, size):
    whole = jnp.zeros((size,) + values.shape, values.dtype)
    for place, part in shifts(values, axis, size):
        whole = lax.dynamic_update_index_in_dim(whole, part, place, 0)
    return whole


def line_parts(parts, axis, size):
    me = lax.axis_index(axis)
    kept = lax.dynamic_index_in_dim(parts, me, 0, keepdims=False)
    theirs = [
        lax.dynamic_index_in_dim(parts, (me + shift) % size, 0, keepdims=False)
        for shift in range(1, size)
    ]
    return kept, theirs


def line_move(theirs, axis, size):
    return [
        lax.ppermute(part, axis, [(i, (i + shift) % size) for i in range(size)])
        for shift, part in enumerate(theirs, 1)
    ]


def line_send(parts, axis, size):
    kept, theirs = line_parts(parts, axis, size)
    return kept, line_move(theirs, axis, size)


def add_up(kept, got):
    total = kept.astype(f32)
    for part in got:
        total = total + part.astype(f32)
    return total


def after(values, earlier):
    return lax.optimization_barrier((values, earlier))[0]


def make_shards(sizes):
    seq = sizes["r"] * sizes["q"]
    dp = sizes["p"] * sizes["c"]
    devices = seq * dp
    heads = H // seq
    wide = heads * HD

    def spread(values, axes):
        return lax.all_to_all(values, axes, 0, 0, tiled=True)

    def shards(
        inputs, cotangent, context, levels, w_qkv, b_qkv, w_out, b_out, w_up, b_up,
        w_down, b_down, w_mod, b_mod,
    ):
        own_frame = lax.axis_index(SEQ)
        core = lax.axis_index("c")
        patches = inputs.shape[1]
        tokens = seq * patches
        own_rows = w_mod.shape[0]

        effective = jnp.where(own_frame < context, 0, levels[:, 0])
        condition = jax.nn.silu(level_embedding(effective, D)).astype(bf16)
        biases = jnp.concatenate([b_qkv, b_out, b_up, b_down, b_mod])
        first = jnp.concatenate(
            [
                condition.reshape(devices, own_rows),
                jnp.broadcast_to(biases, (devices, biases.shape[0])),
            ],
            axis=1,
        )
        first = spread(first, ALL)
        pieces = first[:, :own_rows]
        at = own_rows
        full = []
        for bias in (b_qkv, b_out, b_up, b_down, b_mod):
            size = bias.shape[0]
            full.append(first[:, at : at + size].reshape(-1).astype(f32))
            at += size
        qkv_bias, out_bias, up_bias, down_bias, mod_bias = full
        mod_parts = jnp.dot(pieces, w_mod, preferred_element_type=f32).astype(bf16)
        modulation = jnp.sum(spread(mod_parts, ALL).astype(f32), axis=0) + mod_bias
        scale_attend = modulation[None, D : 2 * D]
        frame_mod = spread(jnp.broadcast_to(modulation[None, : 2 * D], (seq, 2 * D)), SEQ)

        own_qkv = jnp.transpose(w_qkv.reshape(own_rows, 3, seq, wide), (2, 0, 1, 3))
        own_qkv = spread(own_qkv.reshape(seq, own_rows, 3 * wide), SEQ)
        own_qkv = line_gather(line_gather(own_qkv, "c", sizes["c"]), "p", sizes["p"])
        own_qkv = own_qkv.reshape(D, 3 * wide)

        rows = inputs[0]
        clip = lax.all_gather(rows, SEQ, axis=0, tiled=False)

        def whole(weight):
            return lax.all_gather(weight, ALL, axis=0, tiled=True)

        stack = jnp.concatenate(
            [w_down] + [w_up[:, at : at + D] for at in range(0, w_up.shape[1], D)] + [w_out]
        )
        stack = line_gather(stack, "p", sizes["p"])
        stack = lax.all_gather(stack, ("c", "r", "q"), axis=0, tiled=False)
        qkv_weight = whole(after(w_qkv, stack))

        own_bias = lax.dynamic_index_in_dim(
            qkv_bias.reshape(3, seq, wide), own_frame, 1, keepdims=False
        ).reshape(1, 3 * wide)
        token = jnp.arange(tokens)
        patch = token % patches
        angles = rope_angles(token // patches, patch // PW, patch % PW, HD)
        cosine, sine = jnp.cos(angles), jnp.sin(angles)
        cosine = jnp.concatenate([cosine, cosine], axis=-1)
        sine = jnp.concatenate([-sine, sine], axis=-1)
        hidden_all, queries, keys, keys_t, values, values_t = project(
            clip, frame_mod.reshape(seq, 2, D), own_qkv, own_bias, cosine, sine, heads
        )
        out_t, attended, lse = attend(queries, keys, values_t, patches)

        attended = spread(attended, SEQ)
        live = (own_frame >= context).astype(f32)[:, None]
        (
            layer_out, middle_grad, activated, up_grad, two_grads, left_halves, attended_grad,
            stats, g_bup,
        ) = middle(
            attended, rows, cotangent[0], modulation.reshape(6, D), live,
            (out_bias[None], down_bias[None], up_bias[None]), stack, sizes["p"],
        )
        gate_attend_grad, shift_feed_grad, scale_feed_grad, gate_feed_grad = (
            stats[i] for i in range(4)
        )
        g_bdown, g_bout = stats[4], stats[5]
        attended_grad = spread(attended_grad, SEQ)

        def both_cores(values):
            mine = lax.dynamic_index_in_dim(values, core, 0, keepdims=False)
            theirs = lax.dynamic_index_in_dim(values, 1 - core, 0, keepdims=False)
            return jnp.concatenate([mine, swap(theirs, "c")])

        two_got = swap(two_grads, "c")
        right = jnp.concatenate([two_grads, two_got], axis=1)
        activated = both_cores(activated)
        left_halves = both_cores(left_halves)
        up_grad = jnp.concatenate([up_grad, swap(up_grad, "c")])

        def by_chip(total):
            return total.astype(bf16).reshape(
                sizes["p"], sizes["r"], sizes["q"], -1, total.shape[1]
            )

        g_down = by_chip(outer_sum(activated, right[0]))
        g_up = by_chip(outer_sum(left_halves[:, : D // 2], up_grad))
        g_out = by_chip(outer_sum(left_halves[:, D // 2 :], right[1]))

        def columns(values, part):
            half = values.shape[-1] // 2
            return values[..., :half] if part == 0 else values[..., half:]

        groups = []
        for arrays in ((g_down,), (g_up, g_out)):
            one = [jnp.moveaxis(columns(values, 0), 2, 0) for values in arrays]
            two = [jnp.moveaxis(columns(values, 1), 2, 1) for values in arrays]
            one, two = (jnp.concatenate(parts, axis=-1) for parts in (one, two))
            groups.append((line_parts(one, "q", sizes["q"]), line_parts(two, "p", sizes["p"])))

        attended_grad = after(attended_grad, groups)
        groups = [
            tuple(
                (kept, line_move(theirs, axis, sizes[axis]))
                for (kept, theirs), axis in zip(group, ("q", "p"))
            )
            for group in groups
        ]
        dqkv = attend_back(
            queries, keys, keys_t, values, attended_grad, out_t, lse, cosine, sine, patches,
        ).reshape(tokens, 3 * wide)
        qkv_got = spread(dqkv.reshape(seq, patches, 3 * wide), SEQ)
        g_own = outer_sum(hidden_all, dqkv).astype(bf16).reshape(
            sizes["p"], sizes["c"], seq, own_rows, 3 * wide
        )
        own_send = line_send(jnp.moveaxis(g_own, 1, 0), "c", sizes["c"])
        seconds = []
        for one, two in groups:
            one, two = (add_up(kept, after(got, dqkv)).astype(bf16) for kept, got in (one, two))
            seconds.append((line_send(one, "p", sizes["p"]), line_send(two, "q", sizes["q"])))
        own_sum = add_up(*own_send).astype(bf16)
        own_sum = add_up(*line_send(own_sum, "p", sizes["p"])).astype(bf16)
        own_sum = own_sum.reshape(sizes["r"], sizes["q"], own_rows, 3 * wide)
        own_kept, own_got = line_send(jnp.moveaxis(own_sum, 1, 0), "q", sizes["q"])
        qkv_got, seconds, own_got = lax.optimization_barrier((qkv_got, seconds, own_got))
        first_q = lax.axis_index("q") == 0
        own_got = own_got[0]
        own_pair = jnp.concatenate(
            [jnp.where(first_q, own_kept, own_got), jnp.where(first_q, own_got, own_kept)],
            axis=-1,
        )
        thirds = []
        for (one, two), more in zip(seconds, ((), (own_pair,))):
            both = jnp.concatenate([add_up(*one), add_up(*two)], axis=-1).astype(bf16)
            thirds.append(line_send(jnp.concatenate((both,) + more, axis=-1), "r", sizes["r"]))

        qkv_grad = jnp.transpose(
            qkv_got.reshape(seq, patches, 3, wide), (1, 2, 0, 3)
        ).reshape(patches, 3 * D)
        g_bqkv = jnp.sum(qkv_grad.astype(f32), axis=0)
        start_rows = rows.astype(f32)
        hidden_grad = back_dot(qkv_grad, qkv_weight)
        normed, inv_std = layer_norm(start_rows)
        scale_attend_grad = jnp.sum(hidden_grad * normed, axis=0)
        shift_attend_grad = jnp.sum(hidden_grad, axis=0)
        input_grad = middle_grad + norm_back(
            normed, inv_std, hidden_grad * (1.0 + scale_attend)
        )

        mod_grad = jnp.concatenate(
            [
                shift_attend_grad, scale_attend_grad, gate_attend_grad,
                shift_feed_grad, scale_feed_grad, gate_feed_grad,
            ]
        ).astype(bf16)
        last = jnp.concatenate(
            [jnp.broadcast_to(mod_grad, (devices, 6 * D))]
            + [g.astype(bf16).reshape(devices, -1) for g in (g_bqkv, g_bout, g_bup, g_bdown)],
            axis=1,
        )
        last_got = spread(last, ALL)
        all_mod = last_got[:, : 6 * D]
        g_wmod = outer_sum(pieces, all_mod)
        device = lax.axis_index(ALL)
        g_bmod = jnp.sum(
            lax.dynamic_index_in_dim(
                all_mod.reshape(devices, devices, -1), device, 1, keepdims=False
            ).astype(f32),
            axis=0,
        )
        bias_sums = jnp.sum(last_got[:, 6 * D :].astype(f32), axis=0)
        at = 0
        sums = []
        for bias in (b_qkv, b_out, b_up, b_down):
            sums.append(bias_sums[at : at + bias.shape[0]])
            at += bias.shape[0]
        thirds = [(kept, after(got, last)) for kept, got in thirds]
        kept, got = thirds[1]
        own_width = 6 * wide
        place = lax.axis_index("r")
        g_wqkv = jnp.zeros((sizes["r"], own_rows, own_width), bf16)
        for shift, part in enumerate([kept] + list(got)):
            g_wqkv = lax.dynamic_update_index_in_dim(
                g_wqkv, part[:, -own_width:], (place - shift) % sizes["r"], 0
            )
        g_wqkv = jnp.transpose(
            g_wqkv.reshape(sizes["r"], own_rows, 2, 3, wide), (1, 3, 0, 2, 4)
        ).reshape(own_rows, 3 * D).astype(f32)
        g_wdown = add_up(*thirds[0])
        second_sum = add_up(kept[:, :-own_width], [part[:, :-own_width] for part in got])
        half_up, half = w_up.shape[1] // 2, second_sum.shape[1] // 2
        g_wup = jnp.concatenate([second_sum[:, :half_up], second_sum[:, half : half + half_up]], axis=1)
        g_wout = jnp.concatenate([second_sum[:, half_up:half], second_sum[:, half + half_up :]], axis=1)
        return (
            layer_out[None].astype(bf16), input_grad[None].astype(bf16),
            g_wqkv, sums[0], g_wout, sums[1], g_wup, sums[2], g_wdown, sums[3], g_wmod, g_bmod,
        )

    return shards


def solution(mesh):
    dp, seq = mesh.shape["dp"], mesh.shape["seq"]
    sizes = {"p": dp // 2, "c": 2, "r": seq // 2, "q": 2}
    fine = Mesh(mesh.devices.reshape(dp // 2, 2, seq // 2, 2), ALL)
    rows = P(("p", "c"), SEQ, None)
    weight, bias = P(ALL, None), P(ALL)
    pairs = (weight, bias)
    return jax.shard_map(
        make_shards(sizes),
        mesh=fine,
        in_specs=(rows, rows, P(("p", "c")), P(("p", "c"), SEQ)) + pairs * 5,
        out_specs=(rows, rows) + pairs * 5,
        check_vma=False,
    )
```

time: 635 us -> 468 us (0.74)
  local copies, waits for them, and re-layouts: 133 us -> 66.9 us
  starting transfers between devices: 131 us -> 70.9 us
  matrix products: 60.7 us -> 20 us
  other arithmetic: 80.2 us -> 42.9 us
  waiting for transfers between devices: 139 us -> 171 us
  Pallas kernels: 63.9 us -> 71 us
    ppermute x33 -> x20, starting transfers between devices: 71.3 us -> 31.6 us  [the longest x17 26.9 us: line_move(): lax.ppermute(part, axis, [(i, (i + shift) % size) for i in range(size)])]
    all_gather x0 -> x2, waiting for transfers between devices: none -> 38.1 us  [the longest x1 38.1 us: shards(): stack = lax.all_gather(stack, ('c', 'r', 'q'), axis=0, tiled=False)]
    ppermute x33 -> x20, waiting for transfers between devices: 118 us -> 80.4 us  [the longest x17 67.3 us: line_move(): lax.ppermute(part, axis, [(i, (i + shift) % size) for i in range(size)])]
    all_to_all x9 -> x8, waiting for transfers between devices: 18.9 us -> 51.6 us  [spread(): return lax.all_to_all(values, axes, 0, 0, tiled=True)]
    dot_general x5 -> x1, matrix products: 23.4 us -> 0.25 us  [shards(): mod_parts = jnp.dot(pieces, w_mod, preferred_element_type=f32).astype(bf16)]
    dynamic_slice x19 -> x0, local copies, waits for them, and re-layouts: 20.6 us -> none  [the longest x3 11.3 us: shared(): mine = lax.dynamic_index_in_dim(parted, core, 2, keepdims=False)]
    reshape x7 -> x3, local copies, waits for them, and re-layouts: 19.9 us -> 0.92 us  [the longest x1 0.85 us: shards(): own_qkv = spread(own_qkv.reshape(seq, own_rows, 3 * wide), SEQ)]
    unnamed x153 -> x142, local copies, waits for them, and re-layouts: 43.6 us -> 26 us
  transfers between devices with their start and end apart: 54 -> 35, of which waited for: 14 -> 12; matrix products, arithmetic and copies ran while one was open for 40% -> 24% of each run, Pallas kernels for 10% -> 10%
where the time goes in v2:
time: 468 us; the launch traced here: 459 us
  waiting for transfers between devices  171 us (37%)
  Pallas kernels  71 us (15%)
  starting transfers between devices  70.9 us (15%)
  local copies, waits for them, and re-layouts  66.9 us (14%)
  other arithmetic  42.9 us (9%)
  matrix products  20 us (4%)
  between operations  16.5 us (4%)
    ppermute x17, waiting for transfers between devices, line_move(): lax.ppermute(part, axis, [(i, (i + shift) % size) for i in range(size)])  67.3 us
    all_to_all x8, waiting for transfers between devices, spread(): return lax.all_to_all(values, axes, 0, 0, tiled=True)  51.6 us
    all_gather x1, waiting for transfers between devices, shards(): stack = lax.all_gather(stack, ('c', 'r', 'q'), axis=0, tiled=False)  38.1 us
    all_to_all x8, starting transfers between devices, spread(): return lax.all_to_all(values, axes, 0, 0, tiled=True)  38 us
    ppermute x17, starting transfers between devices, line_move(): lax.ppermute(part, axis, [(i, (i + shift) % size) for i in range(size)])  26.9 us
    unnamed x142, local copies, waits for them, and re-layouts  26 us
    pallas_call x1, Pallas kernels, attend_back(): pl.pallas_call(lambda *refs: attend_back_kernel(block, heads, frames, *re...  25.1 us
    pallas_call x1, Pallas kernels, middle(): pl.pallas_call(lambda *refs: middle_kernel(parts, tiles, *refs), grid=(ti...  23.3 us
  transfers between devices with their start and end apart: 35, of which 12 were waited for; matrix products, arithmetic and copies ran while one was open for 24% of the time, Pallas kernels for 10%

profile of v2, /device:TPU:0, one launch (start us, length us, event | category | flops | bytes accessed | tf_op | source)
XLA Modules:
  0.0 459.0 jit_solution(826589021031784307)
XLA Ops:
  16.4 13.1 %collective-permute-done.2 = bf16[288,1024]{1,0:T(8,128)(2,1)S(1)} collective-permute-done((bf16[288,1024]{1,0:T(8,128)(2,1)S(1)}, bf16[288,1024]{1,0:T(8,128)(2,1)S(1)}, u32[]{:S(2)}, u32[]{:S(2)}) %collective-permute-start.2) | collective-permute-done | bytes 589856 | tf_op jit(solution)/shard_map/ppermute | solution.py:474
  34.2 6.1 %all-to-all-start = ((bf16[32,2,256]{2,1,0:T(2,128)(2,1)}), bf16[32,2,256]{2,1,0:T(2,128)(2,1)S(1)}, u32[]{:S(2)}, u32[]{:S(2)}) async-start(bf16[32,2,256]{2,1,0:T(2,128)(2,1)} %reshape.359), calls=%async_computation | async-start | bytes 65536 | tf_op jit(solution)/shard_map/all_to_all | solution.py:526
  40.3 9.3 %fusion.45 = (f32[2048,32]{1,0:T(8,128)S(1)}, f32[2048,32]{1,0:T(8,128)S(1)}, f32[2048,32]{1,0:T(8,128)S(1)}) fusion(f32[32]{0:T(128)S(1)} %fusion.66, s32[2048]{0:T(1024)S(1)} %get-tuple-element.151, s32[2048]{0:T(1024)S(1)} %get-tuple-element.152, pred[32]{0:T(512)(128)(4,1)S(1)} %get-tuple-element.153, s32[2048]{0:T(1024)S(1)} %add_select_fusion.2, ...), kind=kLoop, calls=%fused_computation.129 | loop fusion | flops 327680 | bytes 811200 | tf_op jit(solution)/shard_map/neg | solution.py:588
  52.1 5.8 %all-to-all-start.3 = ((bf16[8,32,384]{2,1,0:T(8,128)(2,1)}), bf16[8,32,384]{2,1,0:T(8,128)(2,1)S(1)}, u32[]{:S(2)}, u32[]{:S(2)}) async-start(bf16[8,32,384]{2,1,0:T(8,128)(2,1)} %reshape.317), calls=%async_computation.3 | async-start | bytes 393216 | tf_op jit(solution)/shard_map/all_to_all | solution.py:526
  60.3 11.9 %all-to-all-done.3 = bf16[8,32,384]{2,1,0:T(8,128)(2,1)S(1)} async-done(((bf16[8,32,384]{2,1,0:T(8,128)(2,1)}), bf16[8,32,384]{2,1,0:T(8,128)(2,1)S(1)}, u32[]{:S(2)}, u32[]{:S(2)}) %all-to-all-start.3) | async-done | bytes 196640 | tf_op jit(solution)/shard_map/all_to_all | solution.py:526
  80.7 16.9 %all-to-all-done.1 = bf16[32,2,3072]{2,1,0:T(2,128)(2,1)} async-done(((bf16[32,2,3072]{2,1,0:T(2,128)(2,1)}), bf16[32,2,3072]{2,1,0:T(2,128)(2,1)}, u32[]{:S(2)}, u32[]{:S(2)}) %all-to-all-start.1) | async-done | bytes 393248 | tf_op jit(solution)/shard_map/all_to_all | solution.py:526
  103.7 3.6 all-to-all-start.2
  109.2 5.7 %all-to-all-done.2 = f32[8,1,2048]{2,1,0:T(1,128)S(1)} async-done(((f32[8,1,2048]{2,1,0:T(1,128)}), f32[8,1,2048]{2,1,0:T(1,128)S(1)}, u32[]{:S(2)}, u32[]{:S(2)}) %all-to-all-start.2) | async-done | bytes 65568 | tf_op jit(solution)/shard_map/all_to_all | solution.py:526
  116.4 11.8 %shard_map.229 = (bf16[2048,1024]{1,0:T(8,128)(2,1)S(1)}, bf16[2,2048,64]{2,1,0:T(8,128)(2,1)S(1)}, bf16[2,2048,64]{2,1,0:T(8,128)(2,1)S(1)}, bf16[2,64,2048]{2,...) custom-call(bf16[8,256,1024]{2,1,0:T(8,128)(2,1)} %all-gather.4.cloned.1.call-done.refs_0_, ...), custom_call_target="tpu_custom_call" | custom-call | flops 1 | bytes 1 | tf_op jit(solution)/shard_map/pallas_call | solution.py:128
  131.1 10.8 %shard_map.230 = (f32[2,64,2048]{2,1,0:T(8,128)S(1)}, bf16[8,256,128]{2,1,0:T(8,128)(2,1)}, f32[2,1,2048]{2,1,0:T(1,128)S(1)}) custom-call(bf16[2,2048,64]{2,1,0:T(8,128)(2,1)S(1)} %get-tuple-element.52.refs_0_, bf16[2,2048,64]{2,1,0:T(8,128)(2,1)S(1)} %get-tuple-element.53.refs_1_, bf16[2,64,2048]{2,1,0:T(8,128)(2,1)S(1)} %get-tuple-element.54.refs_2_), custom_call_target="tpu_custom_call" | custom-call | flops 1 | bytes 1 | tf_op jit(solution)/shard_map/pallas_call | solution.py:214
  150.4 17.1 %all-to-all-done.4.refs_0_ = bf16[8,256,128]{2,1,0:T(8,128)(2,1)S(1)} async-done(((bf16[8,256,128]{2,1,0:T(8,128)(2,1)}), bf16[8,256,128]{2,1,0:T(8,128)(2,1)S(1)}, u32[]{:S(2)}, u32[]{:S(2)}) %all-to-all-start.4) | async-done | bytes 524320 | tf_op jit(solution)/shard_map/all_to_all | solution.py:526
  167.5 38.1 %all-gather.6.cloned.1.call-done.refs_8_.refs_9_.refs_10_ = bf16[16,2,288,1024]{3,2,1,0:T(8,128)(2,1)} async-done(((bf16[1,2,288,1024]{3,2,1,0:T(8,128)(2,1)}), bf16[16,2,288,1024]{3,2,1,0:T(8,128)(2,1)}) %all-gather.6.cloned.1.call-update) | async-done | bytes 18874384 | tf_op jit(solution)/shard_map/all_gather | solution.py:577
  205.5 23.3 %shard_map.231 = (bf16[256,1024]{1,0:T(8,128)(2,1)}, f32[256,1024]{1,0:T(8,128)}, bf16[2,256,2048]{2,1,0:T(8,128)(2,1)}, bf16[256,4096]{1,0:T(8,128)(2,1)}, bf16...) custom-call(bf16[8,256,128]{2,1,0:T(8,128)(2,1)} %copy-done.26, ...), custom_call_target="tpu_custom_call" | custom-call | flops 1 | bytes 1 | tf_op jit(solution)/shard_map/pallas_call | solution.py:422
  233.7 7.2 %all-to-all-start.5 = ((bf16[8,256,128]{2,1,0:T(8,128)(2,1)}), bf16[8,256,128]{2,1,0:T(8,128)(2,1)S(1)}, u32[]{:S(2)}, u32[]{:S(2)}) async-start(bf16[8,256,128]{2,1,0:T(8,128)(2,1)} %get-tuple-element.60), calls=%async_computation.5 | async-start | bytes 1048576 | tf_op jit(solution)/shard_map/all_to_all | solution.py:526
  245.5 3.6 convolution_convert_fusion.2
  267.4 25.1 %shard_map.232 = bf16[8,256,384]{2,1,0:T(8,128)(2,1)} custom-call(bf16[2,2048,64]{2,1,0:T(8,128)(2,1)S(1)} %get-tuple-element.52.refs_0_, bf16[2,2048,64]{2,1,0:T(8,128)(2,1)S(1)} %copy-done.5, bf16[2,64,2048]{2,1,0:T(8,128)(2,1)S(1)} %copy-done.13, bf16[2,2048,64]{2,1,0:T(8,128)(2,1)S(1)} %copy-done.9, bf16[8,256,128]{2,1,0:T(8,128)(2,1)S(1)} %all-to-all-done.5.refs_4_, ...), custom_call_target="tpu_custom_call" | custom-call | flops 1 | bytes 1 | tf_op jit(solution)/shard_map/pallas_call | solution.py:292
  292.5 6.0 %all-to-all-start.6 = ((bf16[8,256,384]{2,1,0:T(8,128)(2,1)}), bf16[8,256,384]{2,1,0:T(8,128)(2,1)S(1)}, u32[]{:S(2)}, u32[]{:S(2)}) async-start(bf16[8,256,384]{2,1,0:T(8,128)(2,1)} %shard_map.232), calls=%async_computation.6 | async-start | bytes 3145728 | tf_op jit(solution)/shard_map/all_to_all | solution.py:526
  298.5 4.6 %convolution_convert_fusion.4 = bf16[1024,384]{1,0:T(8,128)(2,1)S(1)} fusion(bf16[2048,1024]{1,0:T(8,128)(2,1)} %copy-done.14, bf16[2048,384]{1,0:T(8,128)(2,1)S(1)} %bitcast.171), kind=kOutput, calls=%fused_computation.34 | convolution fusion | flops 1611005952 | bytes 6553600 | tf_op jit(solution)/shard_map/dot_general | solution.py:69
  309.8 9.8 %collective-permute-done.13 = bf16[2,4,32,2560]{3,2,0,1:T(8,128)(2,1)} collective-permute-done((bf16[2,4,32,2560]{3,2,0,1:T(8,128)(2,1)}, bf16[2,4,32,2560]{3,2,0,1:T(8,128)(2,1)}, u32[]{:S(2)}, u32[]{:S(2)}) %collective-permute-start.13) | collective-permute-done | bytes 1310752 | tf_op jit(solution)/shard_map/ppermute | solution.py:497
  324.6 13.5 %collective-permute-done.11 = bf16[2,4,32,2560]{3,2,1,0:T(8,128)(2,1)} collective-permute-done((bf16[2,4,32,2560]{3,2,1,0:T(8,128)(2,1)}, bf16[2,4,32,2560]{3,2,1,0:T(8,128)(2,1)}, u32[]{:S(2)}, u32[]{:S(2)}) %collective-permute-start.11) | collective-permute-done | bytes 1310752 | tf_op jit(solution)/shard_map/ppermute | solution.py:497
  347.4 20.1 %collective-permute-done.10 = bf16[4,128,512]{2,1,0:T(8,128)(2,1)} collective-permute-done((bf16[4,128,512]{2,1,0:T(8,128)(2,1)}, bf16[4,128,512]{2,1,0:T(8,128)(2,1)}, u32[]{:S(2)}, u32[]{:S(2)}) %collective-permute-start.10) | collective-permute-done | bytes 524320 | tf_op jit(solution)/shard_map/ppermute | solution.py:497
  388.4 6.4 %fusion.25 = (bf16[1024]{0:T(1024)(128)(2,1)S(1)}, f32[256]{0:T(256)}, f32[256]{0:T(256)}, bf16[1024]{0:T(1024)(128)(2,1)S(1)}, f32[256,1024]{1,0:T(8,128)}) fusion(f32[256]{0:T(256)} %add_rsqrt_fusion, f32[256]{0:T(256)S(1)} %copy-done.47, bf16[1,256,1024]{2,1,0:T(8,128)(2,1)S(1)} %copy-done.17, f32[1024]{0:T(1024)S(1)} %copy-done.43, ...), kind=kOutput, calls=%fused_computation.57 | convolution fusion | flops 1613231616 | bytes 9449472 | tf_op jit(solution)/shard_map/dot_general | solution.py:75
  396.4 7.9 %collective-permute-start.22 = (bf16[128,1024]{1,0:T(8,128)(2,1)}, bf16[128,1024]{1,0:T(8,128)(2,1)S(1)}, u32[]{:S(2)}, u32[]{:S(2)}) collective-permute-start(bf16[128,1024]{1,0:T(8,128)(2,1)} %get-tuple-element.126), channel_id=1, source_target_pairs={{0,4},{2,6},{4,0},{6,2},{1,5},{3,7},{5,1},{7,3},{8,12},{10,14},{12... | collective-permute-start | bytes 786440 | tf_op jit(solution)/shard_map/ppermute | solution.py:497
  404.3 20.6 %collective-permute-done.19 = bf16[32,5888]{1,0:T(8,128)(2,1)} collective-permute-done((bf16[32,5888]{1,0:T(8,128)(2,1)}, bf16[32,5888]{1,0:T(8,128)(2,1)}, u32[]{:S(2)}, u32[]{:S(2)}) %collective-permute-start.19) | collective-permute-done | bytes 376864 | tf_op jit(solution)/shard_map/ppermute | solution.py:497
  (323 shorter events, 144.3 us)
Async XLA Ops:
  7.2 108.0 %all-gather.4.cloned.1.call-start = ((), (), s32[]{:S(2)}) async-start(), calls=%async_computation.8 | async-start | bytes 4718592 | tf_op jit(solution)/shard_map/all_gather | solution.py:568
  7.9 197.6 %all-gather.6.cloned.1.call-start = ((), (), s32[]{:S(2)}) async-start(), calls=%async_computation.9 | async-start | bytes 20054016 | tf_op jit(solution)/shard_map/all_gather | solution.py:577
  72.2 25.5 %all-to-all-start.1 = ((bf16[32,2,3072]{2,1,0:T(2,128)(2,1)}), bf16[32,2,3072]{2,1,0:T(2,128)(2,1)}, u32[]{:S(2)}, u32[]{:S(2)}) async-start(bf16[32,2,3072]{2,1,0:T(2,128)(2,1)} %reshape.361), calls=%async_computation.1 | async-start | bytes 786432 | tf_op jit(solution)/shard_map/all_to_all | solution.py:526
  77.9 29.4 %collective-permute-start.1 = (bf16[2,8,32,384]{3,2,1,0:T(8,128)(2,1)}, bf16[2,8,32,384]{3,2,1,0:T(8,128)(2,1)}, u32[]{:S(2)}, u32[]{:S(2)}) collective-permute-start(bf16[2,8,32,384]{3,2,1,0:T(8,128)(2,1)} %bitcast_dynamic-update-slice_fusion.4), channel_id=1, source_target_pairs={{0,16},{16,0},{1,17},{17,1},{2,18},{18,2},{3,19},{19,3},{4,20},{20... | collective-permute-start | bytes 1179656 | tf_op jit(solution)/shard_map/ppermute | solution.py:474
  143.8 23.6 %all-to-all-start.4 = ((bf16[8,256,128]{2,1,0:T(8,128)(2,1)}), bf16[8,256,128]{2,1,0:T(8,128)(2,1)S(1)}, u32[]{:S(2)}, u32[]{:S(2)}) async-start(bf16[8,256,128]{2,1,0:T(8,128)(2,1)} %get-tuple-element.55), calls=%async_computation.4 | async-start | bytes 1048576 | tf_op jit(solution)/shard_map/all_to_all | solution.py:526
  147.3 241.0 %all-gather.8.cloned.1.call-start = ((), (), s32[]{:S(2)}) async-start(), calls=%async_computation.10 | async-start | bytes 6488064 | tf_op jit(solution)/shard_map/all_gather | solution.py:571
  233.7 31.1 %all-to-all-start.5 = ((bf16[8,256,128]{2,1,0:T(8,128)(2,1)}), bf16[8,256,128]{2,1,0:T(8,128)(2,1)S(1)}, u32[]{:S(2)}, u32[]{:S(2)}) async-start(bf16[8,256,128]{2,1,0:T(8,128)(2,1)} %get-tuple-element.60), calls=%async_computation.5 | async-start | bytes 1048576 | tf_op jit(solution)/shard_map/all_to_all | solution.py:526
  251.2 51.9 %collective-permute-start.9 = (bf16[2,4,128,512]{3,2,0,1:T(8,128)(2,1)}, bf16[2,4,128,512]{3,2,0,1:T(8,128)(2,1)}, u32[]{:S(2)}, u32[]{:S(2)}) collective-permute-start(bf16[2,4,128,512]{3,2,0,1:T(8,128)(2,1)} %get-tuple-element.110), channel_id=1, source_target_pairs={{0,16},{16,0},{1,17},{17,1},{2,18},{18,2},{3,19},{19,3},{4,20},{20... | collective-permute-start | bytes 3145736 | tf_op jit(solution)/shard_map/ppermute | solution.py:497
  254.2 49.0 %collective-permute-start.7 = (bf16[2,4,128,512]{3,2,1,0:T(8,128)(2,1)}, bf16[2,4,128,512]{3,2,1,0:T(8,128)(2,1)}, u32[]{:S(2)}, u32[]{:S(2)}) collective-permute-start(bf16[2,4,128,512]{3,2,1,0:T(8,128)(2,1)} %get-tuple-element.112), channel_id=1, source_target_pairs={{0,1},{1,0},{2,3},{3,2},{4,5},{5,4},{6,7},{7,6},{8,9},{9,8},{10,11... | collective-permute-start | bytes 3145736 | tf_op jit(solution)/shard_map/ppermute | solution.py:497
  262.5 57.2 %collective-permute-start.13 = (bf16[2,4,32,2560]{3,2,0,1:T(8,128)(2,1)}, bf16[2,4,32,2560]{3,2,0,1:T(8,128)(2,1)}, u32[]{:S(2)}, u32[]{:S(2)}) collective-permute-start(bf16[2,4,32,2560]{3,2,0,1:T(8,128)(2,1)} %get-tuple-element.106), channel_id=1, source_target_pairs={{0,16},{16,0},{1,17},{17,1},{2,18},{18,2},{3,19},{19,3},{4,20},{20... | collective-permute-start | bytes 3932168 | tf_op jit(solution)/shard_map/ppermute | solution.py:497
  264.7 73.3 %collective-permute-start.11 = (bf16[2,4,32,2560]{3,2,1,0:T(8,128)(2,1)}, bf16[2,4,32,2560]{3,2,1,0:T(8,128)(2,1)}, u32[]{:S(2)}, u32[]{:S(2)}) collective-permute-start(bf16[2,4,32,2560]{3,2,1,0:T(8,128)(2,1)} %get-tuple-element.108), channel_id=1, source_target_pairs={{0,1},{1,0},{2,3},{3,2},{4,5},{5,4},{6,7},{7,6},{8,9},{9,8},{10,11... | collective-permute-start | bytes 3932168 | tf_op jit(solution)/shard_map/ppermute | solution.py:497
  292.5 76.2 %all-to-all-start.6 = ((bf16[8,256,384]{2,1,0:T(8,128)(2,1)}), bf16[8,256,384]{2,1,0:T(8,128)(2,1)S(1)}, u32[]{:S(2)}, u32[]{:S(2)}) async-start(bf16[8,256,384]{2,1,0:T(8,128)(2,1)} %shard_map.232), calls=%async_computation.6 | async-start | bytes 3145728 | tf_op jit(solution)/shard_map/all_to_all | solution.py:526
  306.0 41.4 %collective-permute-start.8 = (bf16[4,128,512]{2,1,0:T(8,128)(2,1)}, bf16[4,128,512]{2,1,0:T(8,128)(2,1)}, u32[]{:S(2)}, u32[]{:S(2)}) collective-permute-start(bf16[4,128,512]{2,1,0:T(8,128)(2,1)} %get-tuple-element.129), channel_id=1, source_target_pairs={{0,16},{16,0},{1,17},{17,1},{2,18},{18,2},{3,19},{19,3},{4,20},{20... | collective-permute-start | bytes 1572872 | tf_op jit(solution)/shard_map/ppermute | solution.py:497
  309.3 35.2 %collective-permute-start.16 = (bf16[8,32,384]{2,1,0:T(8,128)(2,1)S(1)}, bf16[8,32,384]{2,1,0:T(8,128)(2,1)}, u32[]{:S(2)}, u32[]{:S(2)}) collective-permute-start(bf16[8,32,384]{2,1,0:T(8,128)(2,1)S(1)} %dynamic-slice_bitcast_fusion.21), channel_id=1, source_target_pairs={{0,16},{16,0},{1,17},{17,1},{2,18},{18,2},{3,19},{19,3},{4,20},{20... | collective-permute-start | bytes 589832 | tf_op jit(solution)/shard_map/ppermute | solution.py:497
  322.6 46.1 %collective-permute-start.14 = (bf16[4,32,2560]{2,1,0:T(8,128)(2,1)}, bf16[4,32,2560]{2,1,0:T(8,128)(2,1)S(1)}, u32[]{:S(2)}, u32[]{:S(2)}) collective-permute-start(bf16[4,32,2560]{2,1,0:T(8,128)(2,1)} %get-tuple-element.120), channel_id=1, source_target_pairs={{0,1},{1,0},{2,3},{3,2},{4,5},{5,4},{6,7},{7,6},{8,9},{9,8},{10,11... | collective-permute-start | bytes 1966088 | tf_op jit(solution)/shard_map/ppermute | solution.py:497
  341.0 27.7 %collective-permute-start.12 = (bf16[4,32,2560]{2,1,0:T(8,128)(2,1)}, bf16[4,32,2560]{2,1,0:T(8,128)(2,1)S(1)}, u32[]{:S(2)}, u32[]{:S(2)}) collective-permute-start(bf16[4,32,2560]{2,1,0:T(8,128)(2,1)} %get-tuple-element.122), channel_id=1, source_target_pairs={{0,16},{16,0},{1,17},{17,1},{2,18},{18,2},{3,19},{19,3},{4,20},{20... | collective-permute-start | bytes 1966088 | tf_op jit(solution)/shard_map/ppermute | solution.py:497
  342.8 24.7 %collective-permute-start.10 = (bf16[4,128,512]{2,1,0:T(8,128)(2,1)}, bf16[4,128,512]{2,1,0:T(8,128)(2,1)}, u32[]{:S(2)}, u32[]{:S(2)}) collective-permute-start(bf16[4,128,512]{2,1,0:T(8,128)(2,1)} %get-tuple-element.127), channel_id=1, source_target_pairs={{0,1},{1,0},{2,3},{3,2},{4,5},{5,4},{6,7},{7,6},{8,9},{9,8},{10,11... | collective-permute-start | bytes 1572872 | tf_op jit(solution)/shard_map/ppermute | solution.py:497
  345.4 23.2 %collective-permute-start.17 = (bf16[4,32,384]{2,1,0:T(8,128)(2,1)S(1)}, bf16[4,32,384]{2,1,0:T(8,128)(2,1)S(1)}, u32[]{:S(2)}, u32[]{:S(2)}) collective-permute-start(bf16[4,32,384]{2,1,0:T(8,128)(2,1)S(1)} %dynamic-slice_bitcast_fusion.22), channel_id=1, source_target_pairs={{0,1},{1,0},{2,3},{3,2},{4,5},{5,4},{6,7},{7,6},{8,9},{9,8},{10,11... | collective-permute-start | bytes 294920 | tf_op jit(solution)/shard_map/ppermute | solution.py:497
  375.7 20.7 %collective-permute-start.20 = (bf16[32,5888]{1,0:T(8,128)(2,1)}, bf16[32,5888]{1,0:T(8,128)(2,1)}, u32[]{:S(2)}, u32[]{:S(2)}) collective-permute-start(bf16[32,5888]{1,0:T(8,128)(2,1)} %get-tuple-element.116), channel_id=1, source_target_pairs={{0,6},{2,0},{4,2},{6,4},{1,7},{3,1},{5,3},{7,5},{8,14},{10,8},{12,... | collective-permute-start | bytes 1130504 | tf_op jit(solution)/shard_map/ppermute | solution.py:497
  379.2 45.8 %collective-permute-start.19 = (bf16[32,5888]{1,0:T(8,128)(2,1)}, bf16[32,5888]{1,0:T(8,128)(2,1)}, u32[]{:S(2)}, u32[]{:S(2)}) collective-permute-start(bf16[32,5888]{1,0:T(8,128)(2,1)} %get-tuple-element.117), channel_id=1, source_target_pairs={{0,4},{2,6},{4,0},{6,2},{1,5},{3,7},{5,1},{7,3},{8,12},{10,14},{12... | collective-permute-start | bytes 1130504 | tf_op jit(solution)/shard_map/ppermute | solution.py:497
  379.5 45.5 %collective-permute-start.18 = (bf16[32,5888]{1,0:T(8,128)(2,1)}, bf16[32,5888]{1,0:T(8,128)(2,1)}, u32[]{:S(2)}, u32[]{:S(2)}) collective-permute-start(bf16[32,5888]{1,0:T(8,128)(2,1)} %get-tuple-element.118), channel_id=1, source_target_pairs={{0,2},{2,4},{4,6},{6,0},{1,3},{3,5},{5,7},{7,1},{8,10},{10,12},{12... | collective-permute-start | bytes 1130504 | tf_op jit(solution)/shard_map/ppermute | solution.py:497
  383.9 48.1 %collective-permute-start.23 = (bf16[128,1024]{1,0:T(8,128)(2,1)}, bf16[128,1024]{1,0:T(8,128)(2,1)}, u32[]{:S(2)}, u32[]{:S(2)}) collective-permute-start(bf16[128,1024]{1,0:T(8,128)(2,1)} %get-tuple-element.124), channel_id=1, source_target_pairs={{0,6},{2,0},{4,2},{6,4},{1,7},{3,1},{5,3},{7,5},{8,14},{10,8},{12,... | collective-permute-start | bytes 786440 | tf_op jit(solution)/shard_map/ppermute | solution.py:497
  386.8 45.2 %collective-permute-start.21 = (bf16[128,1024]{1,0:T(8,128)(2,1)}, bf16[128,1024]{1,0:T(8,128)(2,1)}, u32[]{:S(2)}, u32[]{:S(2)}) collective-permute-start(bf16[128,1024]{1,0:T(8,128)(2,1)} %get-tuple-element.125), channel_id=1, source_target_pairs={{0,2},{2,4},{4,6},{6,0},{1,3},{3,5},{5,7},{7,1},{8,10},{10,12},{12... | collective-permute-start | bytes 786440 | tf_op jit(solution)/shard_map/ppermute | solution.py:497
  396.4 37.8 %collective-permute-start.22 = (bf16[128,1024]{1,0:T(8,128)(2,1)}, bf16[128,1024]{1,0:T(8,128)(2,1)S(1)}, u32[]{:S(2)}, u32[]{:S(2)}) collective-permute-start(bf16[128,1024]{1,0:T(8,128)(2,1)} %get-tuple-element.126), channel_id=1, source_target_pairs={{0,4},{2,6},{4,0},{6,2},{1,5},{3,7},{5,1},{7,3},{8,12},{10,14},{12... | collective-permute-start | bytes 786440 | tf_op jit(solution)/shard_map/ppermute | solution.py:497
  (72 other events, 780.9 us)
Sparse Core Ops, SparseCore 0:
  10.2 86.7 all-gather.3
  98.5 106.9 all-gather.5
  233.8 107.8 all-gather.7
